TPU v7x, 256 devices: a whole 4x4x8 slice. The times are simulated.
256 devices in a mesh: dp: 256 (over y, z, x, core).
Axes of the slice: x: 4, y: 4, z: 8, core: 2. Of those that a mesh axis runs over, the one named last changes fastest.
Arguments:
- images: float32 [131072, 1152], P('dp'), may hold values from -1.0298836 to 1.0298836
- texts: float32 [131072, 1152], P('dp'), may hold values from -1.0298836 to 1.0298836
- logit_scale: float32 [1], replicated, may hold values from 2 to 6
- logit_bias: float32 [1], replicated, may hold values from -4 to -1
Outputs:
- image_grad: float32 [131072, 1152], P('dp')
- text_grad: float32 [131072, 1152], P('dp')
All inputs are finite; a program needn't handle non-finite values.
Results may differ from a plain program's by a relative error of at most 0.000088.
Values sent between devices are 32-bit elements; how exact they have to be, the bound alone decides.
No kernel may reach another device: no remote copies, remote signals or barrier semaphores. Data moves between devices by JAX's collectives and lax.ppermute only.
A program may use at most 64 MiB of HBM per device.

v0:
```python
import functools

import jax
import jax.numpy as jnp
from jax import lax
from jax.experimental import pallas as pl
from jax.experimental.pallas import tpu as pltpu
from jax.sharding import PartitionSpec as P

F32 = jnp.float32
BF16 = jnp.bfloat16
ANY = pl.BlockSpec(memory_space=pl.ANY)
VMEM = pl.BlockSpec(memory_space=pltpu.VMEM)
VMEM_LIMIT = 20 * 1024 * 1024

HINT = 10

SECOND = (384, 128)
RETURN = (256, 256)
TILE = 256
COLUMNS = 384


def halves(x):
    high = x.astype(BF16)
    return high, (x - high.astype(F32)).astype(BF16)


def dot3(xs, ys, dims):
    def one(x, y):
        return lax.dot_general(x, y, (dims, ((), ())), preferred_element_type=F32)

    return one(xs[0], ys[0]) + (one(xs[0], ys[1]) + one(xs[1], ys[0]))


def sigmoid(x):
    return 1.0 / (1.0 + jnp.exp(-x))


def offsets(rows):
    starts, at = [], 0
    for r in rows:
        starts.append(at)
        at += r
    return starts


def spans(total, tile):
    return [pl.ds(start, tile) for start in range(0, total, tile)]


def is_even():
    return lax.rem(lax.axis_index("dp"), 2) == 0


def wide(*shape):
    return jax.ShapeDtypeStruct(shape, F32)


def thin(*shape):
    return jax.ShapeDtypeStruct(shape, BF16)


def call(kernel, name, args, in_specs, out_shape, out_specs, flops, scratch=(), aliases=None):
    return pl.pallas_call(
        kernel,
        out_shape=out_shape,
        in_specs=in_specs,
        out_specs=out_specs,
        scratch_shapes=list(scratch),
        input_output_aliases=aliases or {},
        compiler_params=pltpu.CompilerParams(vmem_limit_bytes=VMEM_LIMIT),
        cost_estimate=pl.CostEstimate(flops=flops, bytes_accessed=4 * 1024 * 1024, transcendentals=512 * 512),
        name=name,
    )(*args)


def joined(parts, axis):
    return jnp.concatenate(parts, axis=axis)


def one_dot(x, y, dims):
    return lax.dot_general(x, y, (dims, ((), ())), preferred_element_type=F32)


def scores(xs, ys):
    (xh, xl), (yh, yl) = xs, ys
    return one_dot(joined([xh, xh, xl], 1), joined([yh, yl, yh], 1), ((1,), (1,)))


def weighted(cs, ys):
    (ch, cl), (yh, yl) = cs, ys
    return one_dot(joined([ch, ch, cl], 1), joined([yh, yl, yh], 0), ((1,), (0,)))


def coefs(xs, ys, params):
    scale, bias = params[0:1, 0:1], params[8:9, 0:1]
    return halves(scale * sigmoid(scale * scores(xs, ys) + bias))


def term(xs, ys, params):
    return weighted(coefs(xs, ys, params), ys)


def link_side():
    return lax.rem(lax.axis_index("dp"), 2)


def to_output(side, source, targets, sem):
    for k in range(2):
        pl.when(side == k)(pltpu.make_async_copy(source, targets[k], sem).start)


def own_kernel(scale_ref, bias_ref, images, texts, grads, high, low, params):
    for k, block in enumerate((images, texts)):
        high[k], low[k] = halves(block[...])
    scale, bias = scale_ref[...], bias_ref[...]
    params[0:8, :] = jnp.broadcast_to(scale, (8, 128))
    params[8:16, :] = jnp.broadcast_to(bias, (8, 128))
    ys = (high[1], low[1])
    for t, span in enumerate(spans(images.shape[0], TILE)):
        xs = (high[0, span, :], low[0, span, :])
        logits = scale * scores(xs, ys) + bias
        shape = logits.shape
        diagonal = lax.broadcasted_iota(jnp.int32, shape, 0) + t * TILE == (
            lax.broadcasted_iota(jnp.int32, shape, 1)
        )
        sign = jnp.where(diagonal, -1.0, 1.0).astype(F32)
        coef = halves(sign * scale * sigmoid(sign * logits))
        grads[0, span, :] = weighted(coef, ys)
        side = dot3(coef, xs, ((0,), (0,)))
        grads[1] = side if t == 0 else grads[1] + side


def own(images, texts, scale, bias):
    rows, width = images.shape
    return call(
        own_kernel,
        "own_pair",
        (scale.reshape(1, 1), bias.reshape(1, 1), images, texts),
        [VMEM] * 4,
        [wide(2, rows, width), thin(2, rows, width), thin(2, rows, width), wide(16, 128)],
        [VMEM] * 4,
        HINT * 18 * rows * rows * width,
    )


def near_kernel(params, y, high, low, grads, grads_out, yh, yl):
    side = 1 - link_side()
    ys = halves(y[...])
    yh[...], yl[...] = ys
    for span in spans(y.shape[0], TILE):
        xs = (high[side, span, :], low[side, span, :])
        grads_out[side, span, :] = grads[side, span, :] + term(xs, ys, params)


def near(params, y, high, low, grads):
    rows, width = y.shape
    return call(
        near_kernel,
        "near_pair",
        (params, y, high, low, grads),
        [VMEM] * 5,
        [wide(2, rows, width)] + [thin(rows, width)] * 2,
        [VMEM] * 3,
        12 * rows * rows * width,
        aliases={4: 0},
    )


def mate_kernel(params, xh, xl, y, *refs):
    outs, (yh, yl) = refs[:-2], refs[-2:]
    ys = halves(y[...])
    yh[...], yl[...] = ys
    for start, out in zip(offsets([out.shape[0] for out in outs]), outs):
        span = pl.ds(start, out.shape[0])
        out[...] = term((xh[span, :], xl[span, :]), ys, params)


def mate(params, xh, xl, y):
    rows, width = xh.shape
    return call(
        mate_kernel,
        "mate_pair",
        (params, xh, xl, y),
        [VMEM] * 4,
        [wide(r, width) for r in RETURN] + [thin(rows, width)] * 2,
        [VMEM] * (len(RETURN) + 2),
        12 * rows * rows * width,
    )


def link_kernel(params, yh, yl, high, low, grads, grads_out):
    side = link_side()
    ys = (yh[...], yl[...])
    for span in spans(yh.shape[0], TILE):
        xs = (high[side, span, :], low[side, span, :])
        grads_out[side, span, :] = grads[side, span, :] + term(xs, ys, params)


def link(params, ys, high, low, grads):
    _, rows, width = grads.shape
    return call(
        link_kernel,
        "link_pair",
        (params, *ys, high, low, grads),
        [VMEM] * 6,
        wide(2, rows, width),
        VMEM,
        12 * rows * rows * width,
        aliases={5: 0},
    )


def far_kernel(nr, params, y, *refs):
    terms, (high, low, grads, grads_out, images_out, texts_out, result, sems) = refs[:nr], refs[nr:]
    side = link_side()
    starts = offsets([piece.shape[0] for piece in terms])
    for i, (start, piece) in enumerate(zip(starts, terms)):
        span = pl.ds(start, piece.shape[0])
        result[span, :] = grads[1 - side, span, :] + piece[...]
        to_output(1 - side, result.at[span], (images_out.at[span], texts_out.at[span]), sems.at[i])
    ys = halves(y[...])
    for span in spans(grads.shape[1], TILE):
        xs = (high[side, span, :], low[side, span, :])
        grads_out[side, span, :] = grads[side, span, :] + term(xs, ys, params)
    for i, (start, piece) in enumerate(zip(starts, terms)):
        span = pl.ds(start, piece.shape[0])
        pltpu.make_async_copy(result.at[span], images_out.at[span], sems.at[i]).wait()


def far(params, y, terms, high, low, grads):
    _, rows, width = grads.shape
    first = 2 + len(terms) + 2
    return call(
        functools.partial(far_kernel, len(terms)),
        "far_pair",
        (params, y, *terms, high, low, grads),
        [VMEM] * (first + 1),
        [wide(2, rows, width)] + [wide(rows, width)] * 2,
        [VMEM, ANY, ANY],
        12 * rows * y.shape[0] * width,
        [pltpu.VMEM((rows, width), F32), pltpu.SemaphoreType.DMA((len(terms),))],
        {first: 0},
    )


def last_kernel(params, y, high, low, grads, images_in, texts_in, images_out, texts_out, result, sems):
    side = link_side()
    yh, yl = halves(y[...])
    depth, width = y.shape
    xh, xl = high[side], low[side]
    both = one_dot(xh, joined([yh, yl], 0), ((1,), (1,)))
    total = both[:, :depth] + both[:, depth:] + one_dot(xl, yh, ((1,), (1,)))
    scale, bias = params[0:1, 0:1], params[8:9, 0:1]
    ch, cl = halves(scale * sigmoid(scale * total + bias))
    cs = joined([ch, cl, ch], 1)
    for i, start in enumerate(range(0, width, COLUMNS)):
        span = pl.ds(start, COLUMNS)
        yc = joined([yh[:, start : start + COLUMNS]] * 2 + [yl[:, start : start + COLUMNS]], 0)
        result[:, span] = grads[side, :, span] + one_dot(cs, yc, ((1,), (0,)))
        to_output(side, result.at[:, span], (images_out.at[:, span], texts_out.at[:, span]), sems.at[i])
    for i, start in enumerate(range(0, width, COLUMNS)):
        span = pl.ds(start, COLUMNS)
        pltpu.make_async_copy(result.at[:, span], images_out.at[:, span], sems.at[i]).wait()


def last(params, y, high, low, grads, outs):
    _, rows, width = grads.shape
    return call(
        last_kernel,
        "last_pair",
        (params, y, high, low, grads, *outs),
        [VMEM] * 5 + [ANY] * 2,
        [wide(rows, width)] * 2,
        [ANY] * 2,
        12 * rows * y.shape[0] * width,
        [pltpu.VMEM((rows, width), F32), pltpu.SemaphoreType.DMA((width // COLUMNS,))],
        {5: 0, 6: 1},
    )


def after(value, *earlier):
    return lax.optimization_barrier((value, earlier))[0]


def body(images, texts, scale, bias):
    peers = lax.axis_size("dp")

    def over_link(x):
        return lax.ppermute(
            x, "dp", [(i, (i + 1) % peers if i % 2 else (i - 1) % peers) for i in range(peers)]
        )

    def on_chip(x):
        return lax.ppermute(x, "dp", [(i, i ^ 1) for i in range(peers)])

    even = is_even()
    a = jnp.where(even, images, texts)
    b = jnp.where(even, *after((texts, images), a))
    a1 = over_link(a)
    b1 = on_chip(b)
    grads, high, low, params = own(*after((images, texts), b), scale, bias)
    b1 = after(b1, grads)
    a2 = [over_link(b1[s : s + r]) for s, r in zip(offsets(SECOND), SECOND)]
    grads, bh, bl = near(params, b1, high, low, grads)
    *terms, ah, al = mate(params, bh, bl, after(a1, grads))
    terms = [on_chip(x) for x in terms]
    grads = link(params, (ah, al), high, low, grads)
    grads, *outs = far(params, after(a2[0], grads), terms, high, low, grads)
    return tuple(last(params, after(a2[1], grads), high, low, grads, outs))


def solution(mesh):
    in_specs = (P("dp", None), P("dp", None), P(), P())
    out_specs = (P("dp", None), P("dp", None))
    return jax.shard_map(body, mesh=mesh, in_specs=in_specs, out_specs=out_specs, check_vma=False)
```

profile of v0, /device:TPU:0, one launch (start us, length us, event | category | flops | bytes accessed | tf_op | source)
XLA Modules:
  0.0 65.6 jit_solution(9718737972097554419)
XLA Ops:
  0.6 0.0 copy-start
  0.6 0.0 copy-start.1
  0.7 2.1 %broadcast_select_fusion.1 = f32[512,1152]{1,0:T(8,128)S(1)} fusion(f32[512,1152]{1,0:T(8,128)} %images, f32[512,1152]{1,0:T(8,128)} %texts, pred[]{:T(512)S(6)} %eq.3), kind=kLoop, calls=%fused_computation.1 | loop fusion | flops 589824 | bytes 7077889 | tf_op jit(solution)/shard_map/jit(_where)/select_n | solution.py:299
  2.7 8.3 %collective-permute-start.3 = (f32[512,1152]{1,0:T(8,128)S(1)}, f32[512,1152]{1,0:T(8,128)S(1)}, u32[]{:S(2)}, u32[]{:S(2)}) collective-permute-start(f32[512,1152]{1,0:T(8,128)S(1)} %broadcast_select_fusion.1), channel_id=1, source_target_pairs={{0,255},{1,2},{2,1},{3,4},{4,3},{5,6},{6,5},{7,8},{8,7},{9,10},{10... | collective-permute-start | bytes 7077896 | tf_op jit(solution)/shard_map/ppermute | solution.py:291
  11.0 0.0 copy-done
  11.0 0.0 copy-done.1
  11.0 0.2 broadcast_select_fusion
  11.3 0.1 collective-permute-start
  12.7 6.6 %own_pair.1 = (f32[2,512,1152]{2,1,0:T(8,128)S(1)}, bf16[2,512,1152]{2,1,0:T(8,128)(2,1)S(1)}, bf16[2,512,1152]{2,1,0:T(8,128)(2,1)S(1)}, f32[16,128]{1,0:T(8,128)S(1)}) custom-call(f32[1,1]{1,0:T(1,128)} %bitcast.2.scale_ref, f32[1,1]{1,0:T(1,128)} %bitcast.3.bias_ref, f32[512,1152]{1,0:T(8,128)S(1)} %copy-done, f32[512,1152]{1,0:T(8,128)S(1)} %copy-done.1), custom_call_target="tpu_custom_call" | custom-call | flops 54358179840 | bytes 4194304 | tf_op jit(solution)/shard_map/own_pair/pallas_call | solution.py:65
  19.3 0.0 collective-permute-done.y
  19.3 0.1 slice.7
  19.4 1.8 %collective-permute-start.2 = (f32[384,1152]{1,0:T(8,128)S(1)}, f32[384,1152]{1,0:T(8,128)S(1)}, u32[]{:S(2)}, u32[]{:S(2)}) collective-permute-start(f32[384,1152]{1,0:T(8,128)S(1)} %slice.7), channel_id=1, source_target_pairs={{0,255},{1,2},{2,1},{3,4},{4,3},{5,6},{6,5},{7,8},{8,7},{9,10},{10... | collective-permute-start | bytes 5308424 | tf_op jit(solution)/shard_map/ppermute | solution.py:291
  21.3 4.7 %near_pair.1 = (f32[2,512,1152]{2,1,0:T(8,128)S(1)}, bf16[512,1152]{1,0:T(8,128)(2,1)S(1)}, bf16[512,1152]{1,0:T(8,128)(2,1)S(1)}) custom-call(f32[16,128]{1,0:T(8,128)S(1)} %get-tuple-element.28.params, f32[512,1152]{1,0:T(8,128)S(1)} %collective-permute-done.y, ...), custom_call_target="tpu_custom_call", output_to_operand_aliasing={{0}: (4, {})} | custom-call | flops 3623878656 | bytes 4194304 | tf_op jit(solution)/shard_map/near_pair/pallas_call | solution.py:65
  25.9 11.6 %collective-permute-done.3.y = f32[512,1152]{1,0:T(8,128)S(1)} collective-permute-done((f32[512,1152]{1,0:T(8,128)S(1)}, f32[512,1152]{1,0:T(8,128)S(1)}, u32[]{:S(2)}, u32[]{:S(2)}) %collective-permute-start.3) | collective-permute-done | bytes 2359328 | tf_op jit(solution)/shard_map/ppermute | solution.py:291
  37.6 4.6 %mate_pair.1 = (f32[256,1152]{1,0:T(8,128)S(1)}, f32[256,1152]{1,0:T(8,128)S(1)}, bf16[512,1152]{1,0:T(8,128)(2,1)S(1)}, bf16[512,1152]{1,0:T(8,128)(2,1)S(1)}) custom-call(f32[16,128]{1,0:T(8,128)S(1)} %get-tuple-element.28.params, bf16[512,1152]{1,0:T(8,128)(2,1)S(1)} %get-tuple-element.33.xh, bf16[512,1152]{1,0:T(8,128)(2,1)S(1)} %get-tuple-element.34.xl, ...), custom_call_target="tpu_custom_call" | custom-call | flops 3623878656 | bytes 4194304 | tf_op jit(solution)/shard_map/mate_pair/pallas_call | solution.py:65
  42.1 0.1 collective-permute-start.4
  42.2 0.5 collective-permute-start.5
  42.8 7.5 %collective-permute-start.1 = (f32[128,1152]{1,0:T(8,128)S(1)}, f32[128,1152]{1,0:T(8,128)S(1)}, u32[]{:S(2)}, u32[]{:S(2)}) collective-permute-start(f32[128,1152]{1,0:T(8,128)S(1)} %slice.6), channel_id=1, source_target_pairs={{0,255},{1,2},{2,1},{3,4},{4,3},{5,6},{6,5},{7,8},{8,7},{9,10},{10... | collective-permute-start | bytes 1769480 | tf_op jit(solution)/shard_map/ppermute | solution.py:291
  50.2 4.5 %link_pair.1.refs_4_ = f32[2,512,1152]{2,1,0:T(8,128)S(1)} custom-call(f32[16,128]{1,0:T(8,128)S(1)} %get-tuple-element.28.params, bf16[512,1152]{1,0:T(8,128)(2,1)S(1)} %get-tuple-element.37.yh, bf16[512,1152]{1,0:T(8,128)(2,1)S(1)} %get-tuple-element.38.yl, ...), custom_call_target="tpu_custom_call", output_to_operand_aliasing={{}: (5, {})} | custom-call | flops 3623878656 | bytes 4194304 | tf_op jit(solution)/shard_map/link_pair/pallas_call | solution.py:65
  54.8 1.7 %collective-permute-done.2.y = f32[384,1152]{1,0:T(8,128)S(1)} collective-permute-done((f32[384,1152]{1,0:T(8,128)S(1)}, f32[384,1152]{1,0:T(8,128)S(1)}, u32[]{:S(2)}, u32[]{:S(2)}) %collective-permute-start.2) | collective-permute-done | bytes 1769504 | tf_op jit(solution)/shard_map/ppermute | solution.py:291
  56.5 0.0 collective-permute-done.4.refs_0_
  56.5 0.0 collective-permute-done.5.refs_1_
  56.5 5.7 %far_pair.1 = (f32[2,512,1152]{2,1,0:T(8,128)S(1)}, f32[512,1152]{1,0:T(8,128)}, f32[512,1152]{1,0:T(8,128)}) custom-call(f32[16,128]{1,0:T(8,128)S(1)} %get-tuple-element.28.params, f32[384,1152]{1,0:T(8,128)S(1)} %collective-permute-done.2.y, f32[256,1152]{1,0:T(8,128)S(1)} %collective-permute-done.4.refs_0_, ...), custom_call_target="tpu_custom_call", output_to_operand_aliasing={{0}: (6, {})} | custom-call | flops 2717908992 | bytes 4194304 | tf_op jit(solution)/shard_map/far_pair/pallas_call | solution.py:65
  62.2 0.6 collective-permute-done.1.y
  62.8 2.6 %last_pair.1 = (f32[512,1152]{1,0:T(8,128)}, f32[512,1152]{1,0:T(8,128)}) custom-call(f32[16,128]{1,0:T(8,128)S(1)} %get-tuple-element.28.params, f32[128,1152]{1,0:T(8,128)S(1)} %collective-permute-done.1.y, bf16[2,512,1152]{2,1,0:T(8,128)(2,1)S(1)} %get-tuple-element.31.high.refs_2_, ...), custom_call_target="tpu_custom_call", output_to_operand_aliasing={{0}: (5, {}), {1}: (6, {})} | custom-call | flops 905969664 | bytes 4194304 | tf_op jit(solution)/shard_map/last_pair/pallas_call | solution.py:65
  (1 shorter events, 0.0 us)
Async XLA Ops:
  0.6 10.4 %copy-start = (f32[512,1152]{1,0:T(8,128)S(1)}, f32[512,1152]{1,0:T(8,128)}, u32[]{:S(2)}) copy-start(f32[512,1152]{1,0:T(8,128)} %images) | copy-start | bytes 7077892
  0.6 10.4 %copy-start.1 = (f32[512,1152]{1,0:T(8,128)S(1)}, f32[512,1152]{1,0:T(8,128)}, u32[]{:S(2)}) copy-start(f32[512,1152]{1,0:T(8,128)} %texts) | copy-start | bytes 7077892
  2.7 34.8 %collective-permute-start.3 = (f32[512,1152]{1,0:T(8,128)S(1)}, f32[512,1152]{1,0:T(8,128)S(1)}, u32[]{:S(2)}, u32[]{:S(2)}) collective-permute-start(f32[512,1152]{1,0:T(8,128)S(1)} %broadcast_select_fusion.1), channel_id=1, source_target_pairs={{0,255},{1,2},{2,1},{3,4},{4,3},{5,6},{6,5},{7,8},{8,7},{9,10},{10... | collective-permute-start | bytes 7077896 | tf_op jit(solution)/shard_map/ppermute | solution.py:291
  11.3 8.0 %collective-permute-start = (f32[512,1152]{1,0:T(8,128)S(1)}, f32[512,1152]{1,0:T(8,128)S(1)}, u32[]{:S(2)}, u32[]{:S(2)}) collective-permute-start(f32[512,1152]{1,0:T(8,128)S(1)} %broadcast_select_fusion), channel_id=1, source_target_pairs={{0,1},{1,0},{2,3},{3,2},{4,5},{5,4},{6,7},{7,6},{8,9},{9,8},{10,11... | collective-permute-start | bytes 7077896 | tf_op jit(solution)/shard_map/ppermute | solution.py:296
  19.4 37.1 %collective-permute-start.2 = (f32[384,1152]{1,0:T(8,128)S(1)}, f32[384,1152]{1,0:T(8,128)S(1)}, u32[]{:S(2)}, u32[]{:S(2)}) collective-permute-start(f32[384,1152]{1,0:T(8,128)S(1)} %slice.7), channel_id=1, source_target_pairs={{0,255},{1,2},{2,1},{3,4},{4,3},{5,6},{6,5},{7,8},{8,7},{9,10},{10... | collective-permute-start | bytes 5308424 | tf_op jit(solution)/shard_map/ppermute | solution.py:291
  42.1 14.4 %collective-permute-start.4 = (f32[256,1152]{1,0:T(8,128)S(1)}, f32[256,1152]{1,0:T(8,128)S(1)}, u32[]{:S(2)}, u32[]{:S(2)}) collective-permute-start(f32[256,1152]{1,0:T(8,128)S(1)} %get-tuple-element.40), channel_id=1, source_target_pairs={{0,1},{1,0},{2,3},{3,2},{4,5},{5,4},{6,7},{7,6},{8,9},{9,8},{10,11... | collective-permute-start | bytes 3538952 | tf_op jit(solution)/shard_map/ppermute | solution.py:296
  42.2 14.3 %collective-permute-start.5 = (f32[256,1152]{1,0:T(8,128)S(1)}, f32[256,1152]{1,0:T(8,128)S(1)}, u32[]{:S(2)}, u32[]{:S(2)}) collective-permute-start(f32[256,1152]{1,0:T(8,128)S(1)} %get-tuple-element.41), channel_id=1, source_target_pairs={{0,1},{1,0},{2,3},{3,2},{4,5},{5,4},{6,7},{7,6},{8,9},{9,8},{10,11... | collective-permute-start | bytes 3538952 | tf_op jit(solution)/shard_map/ppermute | solution.py:296
  42.8 20.1 %collective-permute-start.1 = (f32[128,1152]{1,0:T(8,128)S(1)}, f32[128,1152]{1,0:T(8,128)S(1)}, u32[]{:S(2)}, u32[]{:S(2)}) collective-permute-start(f32[128,1152]{1,0:T(8,128)S(1)} %slice.6), channel_id=1, source_target_pairs={{0,255},{1,2},{2,1},{3,4},{4,3},{5,6},{6,5},{7,8},{8,7},{9,10},{10... | collective-permute-start | bytes 1769480 | tf_op jit(solution)/shard_map/ppermute | solution.py:291
where the time goes:
time: 65.7 us; the launch traced here: 65.6 us
  Pallas kernels  28.7 us (44%)
  starting transfers between devices  18.3 us (28%)
  waiting for transfers between devices  14 us (21%)
  other arithmetic  2.32 us (4%)
  between operations  2.21 us (3%)
    pallas_call x6, Pallas kernels, call(): pl.pallas_call(kernel, out_shape=out_shape, in_specs=in_specs, out_specs=...  28.7 us
    ppermute x3, starting transfers between devices, over_link(): lax.ppermute(x, 'dp', [(i, (i + 1) % peers if i % 2 else (i - 1) % peers)...  17.6 us
    ppermute x3, waiting for transfers between devices, over_link(): lax.ppermute(x, 'dp', [(i, (i + 1) % peers if i % 2 else (i - 1) % peers)...  13.9 us
    select_n x1, other arithmetic, body(): a = jnp.where(even, images, texts)  2.07 us
  transfers between devices with their start and end apart: 6, of which 3 were waited for; matrix products, arithmetic and copies ran while one was open for 1% of the time, Pallas kernels for 40%

commit v1 on v0

--- a/solution.py
+++ b/solution.py
@@ -10,11 +10,13 @@
 F32 = jnp.float32
 BF16 = jnp.bfloat16
 ANY = pl.BlockSpec(memory_space=pl.ANY)
+HBM = pl.BlockSpec(memory_space=pltpu.HBM)
 VMEM = pl.BlockSpec(memory_space=pltpu.VMEM)
 VMEM_LIMIT = 20 * 1024 * 1024
 
 HINT = 10
 
+FIRST = (512,)
 SECOND = (384, 128)
 RETURN = (256, 256)
 TILE = 256
@@ -47,10 +49,6 @@
 
 def spans(total, tile):
     return [pl.ds(start, tile) for start in range(0, total, tile)]
-
-
-def is_even():
-    return lax.rem(lax.axis_index("dp"), 2) == 0
 
 
 def wide(*shape):
@@ -102,24 +100,62 @@
     return weighted(coefs(xs, ys, params), ys)
 
 
-def link_side():
-    return lax.rem(lax.axis_index("dp"), 2)
-
-
-def to_output(side, source, targets, sem):
-    for k in range(2):
-        pl.when(side == k)(pltpu.make_async_copy(source, targets[k], sem).start)
-
-
-def own_kernel(scale_ref, bias_ref, images, texts, grads, high, low, params):
-    for k, block in enumerate((images, texts)):
-        high[k], low[k] = halves(block[...])
+LINK, CHIP = 0, 1
+
+
+def by_parity(link_is_images, link_is_texts):
+    even = lax.rem(lax.axis_index("dp"), 2) == 0
+    pl.when(even)(link_is_images)
+    pl.when(jnp.logical_not(even))(link_is_texts)
+
+
+def to_output(side, source, images, texts, sem):
+    first, second = (images, texts) if side == LINK else (texts, images)
+    by_parity(
+        pltpu.make_async_copy(source, first, sem).start,
+        pltpu.make_async_copy(source, second, sem).start,
+    )
+
+
+def pick_kernel(side, start, images, texts, *refs):
+    out, sem = refs[-2:]
+    span = pl.ds(start, out.shape[0])
+    first, second = (images, texts) if side == LINK else (texts, images)
+    by_parity(
+        pltpu.make_async_copy(first.at[span], out, sem).start,
+        pltpu.make_async_copy(second.at[span], out, sem).start,
+    )
+    pltpu.make_async_copy(images.at[span], out, sem).wait()
+
+
+def in_hbm(x):
+    return pltpu.with_memory_space_constraint(x, pltpu.HBM)
+
+
+def pick(side, start, rows, images, texts, *earlier):
+    width = images.shape[1]
+    return call(
+        functools.partial(pick_kernel, side, start),
+        "pick",
+        (in_hbm(images), in_hbm(texts), *earlier),
+        [HBM] * 2 + [ANY] * len(earlier),
+        wide(rows, width),
+        VMEM,
+        0,
+        [pltpu.SemaphoreType.DMA(())],
+    )
+
+
+def own_kernel(scale_ref, bias_ref, chip_block, *refs):
+    link_rows, (grads, high, low, params) = refs[:-4], refs[-4:]
+    high[CHIP], low[CHIP] = halves(chip_block[...])
+    high[LINK], low[LINK] = halves(joined([x[...] for x in link_rows], 0))
     scale, bias = scale_ref[...], bias_ref[...]
     params[0:8, :] = jnp.broadcast_to(scale, (8, 128))
     params[8:16, :] = jnp.broadcast_to(bias, (8, 128))
-    ys = (high[1], low[1])
-    for t, span in enumerate(spans(images.shape[0], TILE)):
-        xs = (high[0, span, :], low[0, span, :])
+    ys = (high[CHIP], low[CHIP])
+    for t, span in enumerate(spans(chip_block.shape[0], TILE)):
+        xs = (high[LINK, span, :], low[LINK, span, :])
         logits = scale * scores(xs, ys) + bias
         shape = logits.shape
         diagonal = lax.broadcasted_iota(jnp.int32, shape, 0) + t * TILE == (
@@ -127,18 +163,18 @@
         )
         sign = jnp.where(diagonal, -1.0, 1.0).astype(F32)
         coef = halves(sign * scale * sigmoid(sign * logits))
-        grads[0, span, :] = weighted(coef, ys)
-        side = dot3(coef, xs, ((0,), (0,)))
-        grads[1] = side if t == 0 else grads[1] + side
-
-
-def own(images, texts, scale, bias):
-    rows, width = images.shape
+        grads[LINK, span, :] = weighted(coef, ys)
+        part = dot3(coef, xs, ((0,), (0,)))
+        grads[CHIP] = part if t == 0 else grads[CHIP] + part
+
+
+def own(link_rows, chip_block, scale, bias):
+    rows, width = chip_block.shape
     return call(
         own_kernel,
         "own_pair",
-        (scale.reshape(1, 1), bias.reshape(1, 1), images, texts),
-        [VMEM] * 4,
+        (scale.reshape(1, 1), bias.reshape(1, 1), chip_block, *link_rows),
+        [VMEM] * (3 + len(link_rows)),
         [wide(2, rows, width), thin(2, rows, width), thin(2, rows, width), wide(16, 128)],
         [VMEM] * 4,
         HINT * 18 * rows * rows * width,
@@ -146,12 +182,11 @@
 
 
 def near_kernel(params, y, high, low, grads, grads_out, yh, yl):
-    side = 1 - link_side()
     ys = halves(y[...])
     yh[...], yl[...] = ys
     for span in spans(y.shape[0], TILE):
-        xs = (high[side, span, :], low[side, span, :])
-        grads_out[side, span, :] = grads[side, span, :] + term(xs, ys, params)
+        xs = (high[CHIP, span, :], low[CHIP, span, :])
+        grads_out[CHIP, span, :] = grads[CHIP, span, :] + term(xs, ys, params)
 
 
 def near(params, y, high, low, grads):
@@ -168,22 +203,22 @@
     )
 
 
-def mate_kernel(params, xh, xl, y, *refs):
-    outs, (yh, yl) = refs[:-2], refs[-2:]
-    ys = halves(y[...])
+def mate_kernel(ny, params, xh, xl, *refs):
+    received, outs, (yh, yl) = refs[:ny], refs[ny:-2], refs[-2:]
+    ys = halves(joined([y[...] for y in received], 0))
     yh[...], yl[...] = ys
     for start, out in zip(offsets([out.shape[0] for out in outs]), outs):
         span = pl.ds(start, out.shape[0])
         out[...] = term((xh[span, :], xl[span, :]), ys, params)
 
 
-def mate(params, xh, xl, y):
+def mate(params, xh, xl, ys):
     rows, width = xh.shape
     return call(
-        mate_kernel,
+        functools.partial(mate_kernel, len(ys)),
         "mate_pair",
-        (params, xh, xl, y),
-        [VMEM] * 4,
+        (params, xh, xl, *ys),
+        [VMEM] * (3 + len(ys)),
         [wide(r, width) for r in RETURN] + [thin(rows, width)] * 2,
         [VMEM] * (len(RETURN) + 2),
         12 * rows * rows * width,
@@ -191,11 +226,10 @@
 
 
 def link_kernel(params, yh, yl, high, low, grads, grads_out):
-    side = link_side()
     ys = (yh[...], yl[...])
     for span in spans(yh.shape[0], TILE):
-        xs = (high[side, span, :], low[side, span, :])
-        grads_out[side, span, :] = grads[side, span, :] + term(xs, ys, params)
+        xs = (high[LINK, span, :], low[LINK, span, :])
+        grads_out[LINK, span, :] = grads[LINK, span, :] + term(xs, ys, params)
 
 
 def link(params, ys, high, low, grads):
@@ -214,16 +248,15 @@
 
 def far_kernel(nr, params, y, *refs):
     terms, (high, low, grads, grads_out, images_out, texts_out, result, sems) = refs[:nr], refs[nr:]
-    side = link_side()
     starts = offsets([piece.shape[0] for piece in terms])
     for i, (start, piece) in enumerate(zip(starts, terms)):
         span = pl.ds(start, piece.shape[0])
-        result[span, :] = grads[1 - side, span, :] + piece[...]
-        to_output(1 - side, result.at[span], (images_out.at[span], texts_out.at[span]), sems.at[i])
+        result[span, :] = grads[CHIP, span, :] + piece[...]
+        to_output(CHIP, result.at[span], images_out.at[span], texts_out.at[span], sems.at[i])
     ys = halves(y[...])
     for span in spans(grads.shape[1], TILE):
-        xs = (high[side, span, :], low[side, span, :])
-        grads_out[side, span, :] = grads[side, span, :] + term(xs, ys, params)
+        xs = (high[LINK, span, :], low[LINK, span, :])
+        grads_out[LINK, span, :] = grads[LINK, span, :] + term(xs, ys, params)
     for i, (start, piece) in enumerate(zip(starts, terms)):
         span = pl.ds(start, piece.shape[0])
         pltpu.make_async_copy(result.at[span], images_out.at[span], sems.at[i]).wait()
@@ -246,10 +279,9 @@
 
 
 def last_kernel(params, y, high, low, grads, images_in, texts_in, images_out, texts_out, result, sems):
-    side = link_side()
     yh, yl = halves(y[...])
     depth, width = y.shape
-    xh, xl = high[side], low[side]
+    xh, xl = high[LINK], low[LINK]
     both = one_dot(xh, joined([yh, yl], 0), ((1,), (1,)))
     total = both[:, :depth] + both[:, depth:] + one_dot(xl, yh, ((1,), (1,)))
     scale, bias = params[0:1, 0:1], params[8:9, 0:1]
@@ -258,8 +290,8 @@
     for i, start in enumerate(range(0, width, COLUMNS)):
         span = pl.ds(start, COLUMNS)
         yc = joined([yh[:, start : start + COLUMNS]] * 2 + [yl[:, start : start + COLUMNS]], 0)
-        result[:, span] = grads[side, :, span] + one_dot(cs, yc, ((1,), (0,)))
-        to_output(side, result.at[:, span], (images_out.at[:, span], texts_out.at[:, span]), sems.at[i])
+        result[:, span] = grads[LINK, :, span] + one_dot(cs, yc, ((1,), (0,)))
+        to_output(LINK, result.at[:, span], images_out.at[:, span], texts_out.at[:, span], sems.at[i])
     for i, start in enumerate(range(0, width, COLUMNS)):
         span = pl.ds(start, COLUMNS)
         pltpu.make_async_copy(result.at[:, span], images_out.at[:, span], sems.at[i]).wait()
@@ -295,12 +327,13 @@
     def on_chip(x):
         return lax.ppermute(x, "dp", [(i, i ^ 1) for i in range(peers)])
 
-    even = is_even()
-    a = jnp.where(even, images, texts)
-    b = jnp.where(even, *after((texts, images), a))
-    a1 = over_link(a)
+    a = []
+    for s, r in zip(offsets(FIRST), FIRST):
+        a.append(pick(LINK, s, r, images, texts, *a))
+    b = pick(CHIP, 0, images.shape[0], images, texts, *a)
+    a1 = [over_link(x) for x in a]
     b1 = on_chip(b)
-    grads, high, low, params = own(*after((images, texts), b), scale, bias)
+    grads, high, low, params = own(a, b, scale, bias)
     b1 = after(b1, grads)
     a2 = [over_link(b1[s : s + r]) for s, r in zip(offsets(SECOND), SECOND)]
     grads, bh, bl = near(params, b1, high, low, grads)

time: 65.7 us -> 65.4 us (level)
  Pallas kernels: 28.7 us -> 32.1 us
  other arithmetic: 2.32 us -> 0 us
  waiting for transfers between devices: 14 us -> 13.2 us
  starting transfers between devices: 18.3 us -> 17.6 us
    pallas_call x6 -> x8, Pallas kernels: 28.7 us -> 32.1 us  [call(): pl.pallas_call(kernel, out_shape=out_shape, in_specs=in_specs, out_specs=...]
    select_n x2 -> x0, other arithmetic: 2.32 us -> none  [the longest x1 2.07 us: body(): a = jnp.where(even, images, texts)]
    ppermute x3, waiting for transfers between devices: 13.9 us -> 13.2 us  [over_link(): lax.ppermute(x, 'dp', [(i, (i + 1) % peers if i % 2 else (i - 1) % peers)...]
  transfers between devices with their start and end apart: 6 -> 6, of which waited for: 3 -> 3; matrix products, arithmetic and copies ran while one was open for 1% -> 0% of each run, Pallas kernels for 40% -> 43%
where the time goes in v1:
time: 65.4 us; the launch traced here: 65.2 us
  Pallas kernels  32.1 us (49%)
  starting transfers between devices  17.6 us (27%)
  waiting for transfers between devices  13.2 us (20%)
  between operations  2.19 us (3%)
    pallas_call x8, Pallas kernels, call(): pl.pallas_call(kernel, out_shape=out_shape, in_specs=in_specs, out_specs=...  32.1 us
    ppermute x3, starting transfers between devices, over_link(): lax.ppermute(x, 'dp', [(i, (i + 1) % peers if i % 2 else (i - 1) % peers)...  17 us
    ppermute x3, waiting for transfers between devices, over_link(): lax.ppermute(x, 'dp', [(i, (i + 1) % peers if i % 2 else (i - 1) % peers)...  13.2 us
  transfers between devices with their start and end apart: 6, of which 3 were waited for; matrix products, arithmetic and copies ran while one was open for 0% of the time, Pallas kernels for 43%

profile of v1, /device:TPU:0, one launch (start us, length us, event | category | flops | bytes accessed | tf_op | source)
XLA Modules:
  0.0 65.2 jit_solution(3530848937937029847)
XLA Ops:
  0.6 1.7 %pick.2.refs_0_ = f32[512,1152]{1,0:T(8,128)S(1)} custom-call(f32[512,1152]{1,0:T(8,128)} %images.3, f32[512,1152]{1,0:T(8,128)} %texts.3), custom_call_target="tpu_custom_call" | custom-call | bytes 4194304 | tf_op jit(solution)/shard_map/pick/pallas_call | solution.py:63
  2.3 8.3 %collective-permute-start.3 = (f32[512,1152]{1,0:T(8,128)S(1)}, f32[512,1152]{1,0:T(8,128)S(1)}, u32[]{:S(2)}, u32[]{:S(2)}) collective-permute-start(f32[512,1152]{1,0:T(8,128)S(1)} %pick.2.refs_0_), channel_id=1, source_target_pairs={{0,255},{1,2},{2,1},{3,4},{4,3},{5,6},{6,5},{7,8},{8,7},{9,10},{10... | collective-permute-start | bytes 7077896 | tf_op jit(solution)/shard_map/ppermute | solution.py:323
  10.6 1.7 %pick.3.chip_block = f32[512,1152]{1,0:T(8,128)S(1)} custom-call(f32[512,1152]{1,0:T(8,128)} %images.3, f32[512,1152]{1,0:T(8,128)} %texts.3, f32[512,1152]{1,0:T(8,128)S(1)} %pick.2.refs_0_), custom_call_target="tpu_custom_call" | custom-call | bytes 4194304 | tf_op jit(solution)/shard_map/pick/pallas_call | solution.py:63
  12.3 0.1 collective-permute-start
  13.7 6.6 %own_pair.1 = (f32[2,512,1152]{2,1,0:T(8,128)S(1)}, bf16[2,512,1152]{2,1,0:T(8,128)(2,1)S(1)}, bf16[2,512,1152]{2,1,0:T(8,128)(2,1)S(1)}, f32[16,128]{1,0:T(8,128)S(1)}) custom-call(f32[1,1]{1,0:T(1,128)} %bitcast.2.scale_ref, f32[1,1]{1,0:T(1,128)} %bitcast.3.bias_ref, f32[512,1152]{1,0:T(8,128)S(1)} %pick.3.chip_block, f32[512,1152]{1,0:T(8,128)S(1)} %pick.2.refs_0_), custom_call_target="tpu_custom_call" | custom-call | flops 54358179840 | bytes 4194304 | tf_op jit(solution)/shard_map/own_pair/pallas_call | solution.py:63
  20.3 0.0 collective-permute-done.y
  20.3 0.1 slice.7
  20.4 1.2 %collective-permute-start.2 = (f32[384,1152]{1,0:T(8,128)S(1)}, f32[384,1152]{1,0:T(8,128)S(1)}, u32[]{:S(2)}, u32[]{:S(2)}) collective-permute-start(f32[384,1152]{1,0:T(8,128)S(1)} %slice.7), channel_id=1, source_target_pairs={{0,255},{1,2},{2,1},{3,4},{4,3},{5,6},{6,5},{7,8},{8,7},{9,10},{10... | collective-permute-start | bytes 5308424 | tf_op jit(solution)/shard_map/ppermute | solution.py:323
  21.6 4.7 %near_pair.1 = (f32[2,512,1152]{2,1,0:T(8,128)S(1)}, bf16[512,1152]{1,0:T(8,128)(2,1)S(1)}, bf16[512,1152]{1,0:T(8,128)(2,1)S(1)}) custom-call(f32[16,128]{1,0:T(8,128)S(1)} %get-tuple-element.20.params, f32[512,1152]{1,0:T(8,128)S(1)} %collective-permute-done.y, ...), custom_call_target="tpu_custom_call", output_to_operand_aliasing={{0}: (4, {})} | custom-call | flops 3623878656 | bytes 4194304 | tf_op jit(solution)/shard_map/near_pair/pallas_call | solution.py:63
  26.3 10.8 %collective-permute-done.3.refs_0_ = f32[512,1152]{1,0:T(8,128)S(1)} collective-permute-done((f32[512,1152]{1,0:T(8,128)S(1)}, f32[512,1152]{1,0:T(8,128)S(1)}, u32[]{:S(2)}, u32[]{:S(2)}) %collective-permute-start.3) | collective-permute-done | bytes 2359328 | tf_op jit(solution)/shard_map/ppermute | solution.py:323
  37.1 4.6 %mate_pair.1 = (f32[256,1152]{1,0:T(8,128)S(1)}, f32[256,1152]{1,0:T(8,128)S(1)}, bf16[512,1152]{1,0:T(8,128)(2,1)S(1)}, bf16[512,1152]{1,0:T(8,128)(2,1)S(1)}) custom-call(f32[16,128]{1,0:T(8,128)S(1)} %get-tuple-element.20.params, bf16[512,1152]{1,0:T(8,128)(2,1)S(1)} %get-tuple-element.25.xh, bf16[512,1152]{1,0:T(8,128)(2,1)S(1)} %get-tuple-element.26.xl, ...), custom_call_target="tpu_custom_call" | custom-call | flops 3623878656 | bytes 4194304 | tf_op jit(solution)/shard_map/mate_pair/pallas_call | solution.py:63
  41.7 0.1 collective-permute-start.4
  41.8 0.5 collective-permute-start.5
  42.4 7.5 %collective-permute-start.1 = (f32[128,1152]{1,0:T(8,128)S(1)}, f32[128,1152]{1,0:T(8,128)S(1)}, u32[]{:S(2)}, u32[]{:S(2)}) collective-permute-start(f32[128,1152]{1,0:T(8,128)S(1)} %slice.6), channel_id=1, source_target_pairs={{0,255},{1,2},{2,1},{3,4},{4,3},{5,6},{6,5},{7,8},{8,7},{9,10},{10... | collective-permute-start | bytes 1769480 | tf_op jit(solution)/shard_map/ppermute | solution.py:323
  49.8 4.6 %link_pair.1.refs_4_ = f32[2,512,1152]{2,1,0:T(8,128)S(1)} custom-call(f32[16,128]{1,0:T(8,128)S(1)} %get-tuple-element.20.params, bf16[512,1152]{1,0:T(8,128)(2,1)S(1)} %get-tuple-element.29.yh, bf16[512,1152]{1,0:T(8,128)(2,1)S(1)} %get-tuple-element.30.yl, ...), custom_call_target="tpu_custom_call", output_to_operand_aliasing={{}: (5, {})} | custom-call | flops 3623878656 | bytes 4194304 | tf_op jit(solution)/shard_map/link_pair/pallas_call | solution.py:63
  54.4 1.7 %collective-permute-done.2.y = f32[384,1152]{1,0:T(8,128)S(1)} collective-permute-done((f32[384,1152]{1,0:T(8,128)S(1)}, f32[384,1152]{1,0:T(8,128)S(1)}, u32[]{:S(2)}, u32[]{:S(2)}) %collective-permute-start.2) | collective-permute-done | bytes 1769504 | tf_op jit(solution)/shard_map/ppermute | solution.py:323
  56.1 0.0 collective-permute-done.4.refs_0_
  56.1 0.0 collective-permute-done.5.refs_1_
  56.1 5.7 %far_pair.1 = (f32[2,512,1152]{2,1,0:T(8,128)S(1)}, f32[512,1152]{1,0:T(8,128)}, f32[512,1152]{1,0:T(8,128)}) custom-call(f32[16,128]{1,0:T(8,128)S(1)} %get-tuple-element.20.params, f32[384,1152]{1,0:T(8,128)S(1)} %collective-permute-done.2.y, f32[256,1152]{1,0:T(8,128)S(1)} %collective-permute-done.4.refs_0_, ...), custom_call_target="tpu_custom_call", output_to_operand_aliasing={{0}: (6, {})} | custom-call | flops 2717908992 | bytes 4194304 | tf_op jit(solution)/shard_map/far_pair/pallas_call | solution.py:63
  61.8 0.6 collective-permute-done.1.y
  62.4 2.6 %last_pair.1 = (f32[512,1152]{1,0:T(8,128)}, f32[512,1152]{1,0:T(8,128)}) custom-call(f32[16,128]{1,0:T(8,128)S(1)} %get-tuple-element.20.params, f32[128,1152]{1,0:T(8,128)S(1)} %collective-permute-done.1.y, bf16[2,512,1152]{2,1,0:T(8,128)(2,1)S(1)} %get-tuple-element.23.high.refs_2_, ...), custom_call_target="tpu_custom_call", output_to_operand_aliasing={{0}: (5, {}), {1}: (6, {})} | custom-call | flops 905969664 | bytes 4194304 | tf_op jit(solution)/shard_map/last_pair/pallas_call | solution.py:63
  (1 shorter events, 0.0 us)
Async XLA Ops:
  2.3 34.8 %collective-permute-start.3 = (f32[512,1152]{1,0:T(8,128)S(1)}, f32[512,1152]{1,0:T(8,128)S(1)}, u32[]{:S(2)}, u32[]{:S(2)}) collective-permute-start(f32[512,1152]{1,0:T(8,128)S(1)} %pick.2.refs_0_), channel_id=1, source_target_pairs={{0,255},{1,2},{2,1},{3,4},{4,3},{5,6},{6,5},{7,8},{8,7},{9,10},{10... | collective-permute-start | bytes 7077896 | tf_op jit(solution)/shard_map/ppermute | solution.py:323
  12.3 8.0 %collective-permute-start = (f32[512,1152]{1,0:T(8,128)S(1)}, f32[512,1152]{1,0:T(8,128)S(1)}, u32[]{:S(2)}, u32[]{:S(2)}) collective-permute-start(f32[512,1152]{1,0:T(8,128)S(1)} %pick.3.chip_block), channel_id=1, source_target_pairs={{0,1},{1,0},{2,3},{3,2},{4,5},{5,4},{6,7},{7,6},{8,9},{9,8},{10,11... | collective-permute-start | bytes 7077896 | tf_op jit(solution)/shard_map/ppermute | solution.py:328
  20.4 35.7 %collective-permute-start.2 = (f32[384,1152]{1,0:T(8,128)S(1)}, f32[384,1152]{1,0:T(8,128)S(1)}, u32[]{:S(2)}, u32[]{:S(2)}) collective-permute-start(f32[384,1152]{1,0:T(8,128)S(1)} %slice.7), channel_id=1, source_target_pairs={{0,255},{1,2},{2,1},{3,4},{4,3},{5,6},{6,5},{7,8},{8,7},{9,10},{10... | collective-permute-start | bytes 5308424 | tf_op jit(solution)/shard_map/ppermute | solution.py:323
  41.7 14.4 %collective-permute-start.4 = (f32[256,1152]{1,0:T(8,128)S(1)}, f32[256,1152]{1,0:T(8,128)S(1)}, u32[]{:S(2)}, u32[]{:S(2)}) collective-permute-start(f32[256,1152]{1,0:T(8,128)S(1)} %get-tuple-element.32), channel_id=1, source_target_pairs={{0,1},{1,0},{2,3},{3,2},{4,5},{5,4},{6,7},{7,6},{8,9},{9,8},{10,11... | collective-permute-start | bytes 3538952 | tf_op jit(solution)/shard_map/ppermute | solution.py:328
  41.8 14.3 %collective-permute-start.5 = (f32[256,1152]{1,0:T(8,128)S(1)}, f32[256,1152]{1,0:T(8,128)S(1)}, u32[]{:S(2)}, u32[]{:S(2)}) collective-permute-start(f32[256,1152]{1,0:T(8,128)S(1)} %get-tuple-element.33), channel_id=1, source_target_pairs={{0,1},{1,0},{2,3},{3,2},{4,5},{5,4},{6,7},{7,6},{8,9},{9,8},{10,11... | collective-permute-start | bytes 3538952 | tf_op jit(solution)/shard_map/ppermute | solution.py:328
  42.4 20.1 %collective-permute-start.1 = (f32[128,1152]{1,0:T(8,128)S(1)}, f32[128,1152]{1,0:T(8,128)S(1)}, u32[]{:S(2)}, u32[]{:S(2)}) collective-permute-start(f32[128,1152]{1,0:T(8,128)S(1)} %slice.6), channel_id=1, source_target_pairs={{0,255},{1,2},{2,1},{3,4},{4,3},{5,6},{6,5},{7,8},{8,7},{9,10},{10... | collective-permute-start | bytes 1769480 | tf_op jit(solution)/shard_map/ppermute | solution.py:323

commit v2 on v1

--- a/solution.py
+++ b/solution.py
@@ -16,7 +16,7 @@
 
 HINT = 10
 
-FIRST = (512,)
+HEAD = 256
 SECOND = (384, 128)
 RETURN = (256, 256)
 TILE = 256
@@ -117,32 +117,34 @@
     )
 
 
-def pick_kernel(side, start, images, texts, *refs):
-    out, sem = refs[-2:]
-    span = pl.ds(start, out.shape[0])
-    first, second = (images, texts) if side == LINK else (texts, images)
-    by_parity(
-        pltpu.make_async_copy(first.at[span], out, sem).start,
-        pltpu.make_async_copy(second.at[span], out, sem).start,
-    )
-    pltpu.make_async_copy(images.at[span], out, sem).wait()
+def pick_kernel(parts, images, texts, *refs):
+    outs, sems = refs[-1 - len(parts) : -1], refs[-1]
+    for k, ((side, start, rows), out) in enumerate(zip(parts, outs)):
+        span = pl.ds(start, rows)
+        first, second = (images, texts) if side == LINK else (texts, images)
+        by_parity(
+            pltpu.make_async_copy(first.at[span], out, sems.at[k]).start,
+            pltpu.make_async_copy(second.at[span], out, sems.at[k]).start,
+        )
+    for k, ((_, start, rows), out) in enumerate(zip(parts, outs)):
+        pltpu.make_async_copy(images.at[pl.ds(start, rows)], out, sems.at[k]).wait()
 
 
 def in_hbm(x):
     return pltpu.with_memory_space_constraint(x, pltpu.HBM)
 
 
-def pick(side, start, rows, images, texts, *earlier):
+def pick(images, texts, parts, *earlier):
     width = images.shape[1]
     return call(
-        functools.partial(pick_kernel, side, start),
+        functools.partial(pick_kernel, parts),
         "pick",
         (in_hbm(images), in_hbm(texts), *earlier),
         [HBM] * 2 + [ANY] * len(earlier),
-        wide(rows, width),
-        VMEM,
+        [wide(rows, width) for _, _, rows in parts],
+        [VMEM] * len(parts),
         0,
-        [pltpu.SemaphoreType.DMA(())],
+        [pltpu.SemaphoreType.DMA((len(parts),))],
     )
 
 
@@ -327,10 +329,10 @@
     def on_chip(x):
         return lax.ppermute(x, "dp", [(i, i ^ 1) for i in range(peers)])
 
-    a = []
-    for s, r in zip(offsets(FIRST), FIRST):
-        a.append(pick(LINK, s, r, images, texts, *a))
-    b = pick(CHIP, 0, images.shape[0], images, texts, *a)
+    rows = images.shape[0]
+    head = pick(images, texts, [(LINK, 0, HEAD)])
+    tail, b = pick(images, texts, [(LINK, HEAD, rows - HEAD), (CHIP, 0, rows)], *head)
+    a = [*head, tail]
     a1 = [over_link(x) for x in a]
     b1 = on_chip(b)
     grads, high, low, params = own(a, b, scale, bias)

time: 65.4 us -> 65 us (level)
  waiting for transfers between devices: 13.2 us -> 6.59 us
  starting transfers between devices: 17.6 us -> 23.9 us
    ppermute x3 -> x4, waiting for transfers between devices: 13.2 us -> 6.58 us  [over_link(): lax.ppermute(x, 'dp', [(i, (i + 1) % peers if i % 2 else (i - 1) % peers)...]
    ppermute x3 -> x4, starting transfers between devices: 17 us -> 23.2 us  [over_link(): lax.ppermute(x, 'dp', [(i, (i + 1) % peers if i % 2 else (i - 1) % peers)...]
  transfers between devices with their start and end apart: 6 -> 7, of which waited for: 3 -> 3; matrix products, arithmetic and copies ran while one was open for 0% -> 0% of each run, Pallas kernels for 43% -> 43%
where the time goes in v2:
time: 65 us; the launch traced here: 64.8 us
  Pallas kernels  32 us (49%)
  starting transfers between devices  23.9 us (37%)
  waiting for transfers between devices  6.59 us (10%)
  between operations  2.2 us (3%)
    pallas_call x8, Pallas kernels, call(): pl.pallas_call(kernel, out_shape=out_shape, in_specs=in_specs, out_specs=...  32 us
    ppermute x4, starting transfers between devices, over_link(): lax.ppermute(x, 'dp', [(i, (i + 1) % peers if i % 2 else (i - 1) % peers)...  23.2 us
    ppermute x4, waiting for transfers between devices, over_link(): lax.ppermute(x, 'dp', [(i, (i + 1) % peers if i % 2 else (i - 1) % peers)...  6.58 us
  transfers between devices with their start and end apart: 7, of which 3 were waited for; matrix products, arithmetic and copies ran while one was open for 0% of the time, Pallas kernels for 43%

profile of v2, /device:TPU:0, one launch (start us, length us, event | category | flops | bytes accessed | tf_op | source)
XLA Modules:
  0.0 64.8 jit_solution(9046224477192946586)
XLA Ops:
  0.6 1.3 %pick.2.refs_0_ = f32[256,1152]{1,0:T(8,128)S(1)} custom-call(f32[512,1152]{1,0:T(8,128)} %images.3, f32[512,1152]{1,0:T(8,128)} %texts.3), custom_call_target="tpu_custom_call" | custom-call | bytes 4194304 | tf_op jit(solution)/shard_map/pick/pallas_call | solution.py:63
  1.9 8.3 %collective-permute-start.3 = (f32[256,1152]{1,0:T(8,128)S(1)}, f32[256,1152]{1,0:T(8,128)S(1)}, u32[]{:S(2)}, u32[]{:S(2)}) collective-permute-start(f32[256,1152]{1,0:T(8,128)S(1)} %pick.2.refs_0_), channel_id=1, source_target_pairs={{0,255},{1,2},{2,1},{3,4},{4,3},{5,6},{6,5},{7,8},{8,7},{9,10},{10... | collective-permute-start | bytes 3538952 | tf_op jit(solution)/shard_map/ppermute | solution.py:325
  10.2 2.0 %pick.3 = (f32[256,1152]{1,0:T(8,128)S(1)}, f32[512,1152]{1,0:T(8,128)S(1)}) custom-call(f32[512,1152]{1,0:T(8,128)} %images.3, f32[512,1152]{1,0:T(8,128)} %texts.3, f32[256,1152]{1,0:T(8,128)S(1)} %pick.2.refs_0_), custom_call_target="tpu_custom_call" | custom-call | bytes 4194304 | tf_op jit(solution)/shard_map/pick/pallas_call | solution.py:63
  12.3 0.1 collective-permute-start.4
  12.4 0.1 collective-permute-start
  13.8 6.6 %own_pair.1 = (f32[2,512,1152]{2,1,0:T(8,128)S(1)}, bf16[2,512,1152]{2,1,0:T(8,128)(2,1)S(1)}, bf16[2,512,1152]{2,1,0:T(8,128)(2,1)S(1)}, f32[16,128]{1,0:T(8,128)S(1)}) custom-call(f32[1,1]{1,0:T(1,128)} %bitcast.2.scale_ref, f32[1,1]{1,0:T(1,128)} %bitcast.3.bias_ref, f32[512,1152]{1,0:T(8,128)S(1)} %get-tuple-element.23.chip_block, ...), custom_call_target="tpu_custom_call" | custom-call | flops 54358179840 | bytes 4194304 | tf_op jit(solution)/shard_map/own_pair/pallas_call | solution.py:63
  20.4 0.0 collective-permute-done.y
  20.4 0.1 slice.7
  20.5 7.3 %collective-permute-start.2 = (f32[384,1152]{1,0:T(8,128)S(1)}, f32[384,1152]{1,0:T(8,128)S(1)}, u32[]{:S(2)}, u32[]{:S(2)}) collective-permute-start(f32[384,1152]{1,0:T(8,128)S(1)} %slice.7), channel_id=1, source_target_pairs={{0,255},{1,2},{2,1},{3,4},{4,3},{5,6},{6,5},{7,8},{8,7},{9,10},{10... | collective-permute-start | bytes 5308424 | tf_op jit(solution)/shard_map/ppermute | solution.py:325
  27.9 4.7 %near_pair.1 = (f32[2,512,1152]{2,1,0:T(8,128)S(1)}, bf16[512,1152]{1,0:T(8,128)(2,1)S(1)}, bf16[512,1152]{1,0:T(8,128)(2,1)S(1)}) custom-call(f32[16,128]{1,0:T(8,128)S(1)} %get-tuple-element.25.params, f32[512,1152]{1,0:T(8,128)S(1)} %collective-permute-done.y, ...), custom_call_target="tpu_custom_call", output_to_operand_aliasing={{0}: (4, {})} | custom-call | flops 3623878656 | bytes 4194304 | tf_op jit(solution)/shard_map/near_pair/pallas_call | solution.py:63
  32.5 0.0 collective-permute-done.3.refs_0_
  32.5 4.2 %collective-permute-done.4.refs_1_ = f32[256,1152]{1,0:T(8,128)S(1)} collective-permute-done((f32[256,1152]{1,0:T(8,128)S(1)}, f32[256,1152]{1,0:T(8,128)S(1)}, u32[]{:S(2)}, u32[]{:S(2)}) %collective-permute-start.4) | collective-permute-done | bytes 1179680 | tf_op jit(solution)/shard_map/ppermute | solution.py:325
  36.7 4.6 %mate_pair.1 = (f32[256,1152]{1,0:T(8,128)S(1)}, f32[256,1152]{1,0:T(8,128)S(1)}, bf16[512,1152]{1,0:T(8,128)(2,1)S(1)}, bf16[512,1152]{1,0:T(8,128)(2,1)S(1)}) custom-call(f32[16,128]{1,0:T(8,128)S(1)} %get-tuple-element.25.params, bf16[512,1152]{1,0:T(8,128)(2,1)S(1)} %get-tuple-element.30.xh, bf16[512,1152]{1,0:T(8,128)(2,1)S(1)} %get-tuple-element.31.xl, ...), custom_call_target="tpu_custom_call" | custom-call | flops 3623878656 | bytes 4194304 | tf_op jit(solution)/shard_map/mate_pair/pallas_call | solution.py:63
  41.3 0.1 collective-permute-start.5
  41.4 0.5 collective-permute-start.6
  41.9 7.5 %collective-permute-start.1 = (f32[128,1152]{1,0:T(8,128)S(1)}, f32[128,1152]{1,0:T(8,128)S(1)}, u32[]{:S(2)}, u32[]{:S(2)}) collective-permute-start(f32[128,1152]{1,0:T(8,128)S(1)} %slice.6), channel_id=1, source_target_pairs={{0,255},{1,2},{2,1},{3,4},{4,3},{5,6},{6,5},{7,8},{8,7},{9,10},{10... | collective-permute-start | bytes 1769480 | tf_op jit(solution)/shard_map/ppermute | solution.py:325
  49.4 4.6 %link_pair.1.refs_4_ = f32[2,512,1152]{2,1,0:T(8,128)S(1)} custom-call(f32[16,128]{1,0:T(8,128)S(1)} %get-tuple-element.25.params, bf16[512,1152]{1,0:T(8,128)(2,1)S(1)} %get-tuple-element.35.yh, bf16[512,1152]{1,0:T(8,128)(2,1)S(1)} %get-tuple-element.36.yl, ...), custom_call_target="tpu_custom_call", output_to_operand_aliasing={{}: (5, {})} | custom-call | flops 3623878656 | bytes 4194304 | tf_op jit(solution)/shard_map/link_pair/pallas_call | solution.py:63
  54.0 1.7 %collective-permute-done.2.y = f32[384,1152]{1,0:T(8,128)S(1)} collective-permute-done((f32[384,1152]{1,0:T(8,128)S(1)}, f32[384,1152]{1,0:T(8,128)S(1)}, u32[]{:S(2)}, u32[]{:S(2)}) %collective-permute-start.2) | collective-permute-done | bytes 1769504 | tf_op jit(solution)/shard_map/ppermute | solution.py:325
  55.7 0.0 collective-permute-done.5.refs_0_
  55.7 0.0 collective-permute-done.6.refs_1_
  55.7 5.7 %far_pair.1 = (f32[2,512,1152]{2,1,0:T(8,128)S(1)}, f32[512,1152]{1,0:T(8,128)}, f32[512,1152]{1,0:T(8,128)}) custom-call(f32[16,128]{1,0:T(8,128)S(1)} %get-tuple-element.25.params, f32[384,1152]{1,0:T(8,128)S(1)} %collective-permute-done.2.y, f32[256,1152]{1,0:T(8,128)S(1)} %collective-permute-done.5.refs_0_, ...), custom_call_target="tpu_custom_call", output_to_operand_aliasing={{0}: (6, {})} | custom-call | flops 2717908992 | bytes 4194304 | tf_op jit(solution)/shard_map/far_pair/pallas_call | solution.py:63
  61.4 0.6 collective-permute-done.1.y
  62.0 2.6 %last_pair.1 = (f32[512,1152]{1,0:T(8,128)}, f32[512,1152]{1,0:T(8,128)}) custom-call(f32[16,128]{1,0:T(8,128)S(1)} %get-tuple-element.25.params, f32[128,1152]{1,0:T(8,128)S(1)} %collective-permute-done.1.y, bf16[2,512,1152]{2,1,0:T(8,128)(2,1)S(1)} %get-tuple-element.28.high.refs_2_, ...), custom_call_target="tpu_custom_call", output_to_operand_aliasing={{0}: (5, {}), {1}: (6, {})} | custom-call | flops 905969664 | bytes 4194304 | tf_op jit(solution)/shard_map/last_pair/pallas_call | solution.py:63
  (1 shorter events, 0.0 us)
Async XLA Ops:
  1.9 30.6 %collective-permute-start.3 = (f32[256,1152]{1,0:T(8,128)S(1)}, f32[256,1152]{1,0:T(8,128)S(1)}, u32[]{:S(2)}, u32[]{:S(2)}) collective-permute-start(f32[256,1152]{1,0:T(8,128)S(1)} %pick.2.refs_0_), channel_id=1, source_target_pairs={{0,255},{1,2},{2,1},{3,4},{4,3},{5,6},{6,5},{7,8},{8,7},{9,10},{10... | collective-permute-start | bytes 3538952 | tf_op jit(solution)/shard_map/ppermute | solution.py:325
  12.3 24.5 %collective-permute-start.4 = (f32[256,1152]{1,0:T(8,128)S(1)}, f32[256,1152]{1,0:T(8,128)S(1)}, u32[]{:S(2)}, u32[]{:S(2)}) collective-permute-start(f32[256,1152]{1,0:T(8,128)S(1)} %get-tuple-element.24.refs_1_), channel_id=1, source_target_pairs={{0,255},{1,2},{2,1},{3,4},{4,3},{5,6},{6,5},{7,8},{8,7},{9,10},{10... | collective-permute-start | bytes 3538952 | tf_op jit(solution)/shard_map/ppermute | solution.py:325
  12.4 8.0 %collective-permute-start = (f32[512,1152]{1,0:T(8,128)S(1)}, f32[512,1152]{1,0:T(8,128)S(1)}, u32[]{:S(2)}, u32[]{:S(2)}) collective-permute-start(f32[512,1152]{1,0:T(8,128)S(1)} %get-tuple-element.23.chip_block), channel_id=1, source_target_pairs={{0,1},{1,0},{2,3},{3,2},{4,5},{5,4},{6,7},{7,6},{8,9},{9,8},{10,11... | collective-permute-start | bytes 7077896 | tf_op jit(solution)/shard_map/ppermute | solution.py:330
  20.5 35.2 %collective-permute-start.2 = (f32[384,1152]{1,0:T(8,128)S(1)}, f32[384,1152]{1,0:T(8,128)S(1)}, u32[]{:S(2)}, u32[]{:S(2)}) collective-permute-start(f32[384,1152]{1,0:T(8,128)S(1)} %slice.7), channel_id=1, source_target_pairs={{0,255},{1,2},{2,1},{3,4},{4,3},{5,6},{6,5},{7,8},{8,7},{9,10},{10... | collective-permute-start | bytes 5308424 | tf_op jit(solution)/shard_map/ppermute | solution.py:325
  41.3 14.4 %collective-permute-start.5 = (f32[256,1152]{1,0:T(8,128)S(1)}, f32[256,1152]{1,0:T(8,128)S(1)}, u32[]{:S(2)}, u32[]{:S(2)}) collective-permute-start(f32[256,1152]{1,0:T(8,128)S(1)} %get-tuple-element.38), channel_id=1, source_target_pairs={{0,1},{1,0},{2,3},{3,2},{4,5},{5,4},{6,7},{7,6},{8,9},{9,8},{10,11... | collective-permute-start | bytes 3538952 | tf_op jit(solution)/shard_map/ppermute | solution.py:330
  41.4 14.3 %collective-permute-start.6 = (f32[256,1152]{1,0:T(8,128)S(1)}, f32[256,1152]{1,0:T(8,128)S(1)}, u32[]{:S(2)}, u32[]{:S(2)}) collective-permute-start(f32[256,1152]{1,0:T(8,128)S(1)} %get-tuple-element.39), channel_id=1, source_target_pairs={{0,1},{1,0},{2,3},{3,2},{4,5},{5,4},{6,7},{7,6},{8,9},{9,8},{10,11... | collective-permute-start | bytes 3538952 | tf_op jit(solution)/shard_map/ppermute | solution.py:330
  41.9 20.1 %collective-permute-start.1 = (f32[128,1152]{1,0:T(8,128)S(1)}, f32[128,1152]{1,0:T(8,128)S(1)}, u32[]{:S(2)}, u32[]{:S(2)}) collective-permute-start(f32[128,1152]{1,0:T(8,128)S(1)} %slice.6), channel_id=1, source_target_pairs={{0,255},{1,2},{2,1},{3,4},{4,3},{5,6},{6,5},{7,8},{8,7},{9,10},{10... | collective-permute-start | bytes 1769480 | tf_op jit(solution)/shard_map/ppermute | solution.py:325

commit v3 on v2

--- a/solution.py
+++ b/solution.py
@@ -17,10 +17,9 @@
 HINT = 10
 
 HEAD = 256
-SECOND = (384, 128)
-RETURN = (256, 256)
+HEAD_TERMS = (256,)
+TAIL_TERMS = (112, 144)
 TILE = 256
-COLUMNS = 384
 
 
 def halves(x):
@@ -183,134 +182,89 @@
     )
 
 
-def near_kernel(params, y, high, low, grads, grads_out, yh, yl):
-    ys = halves(y[...])
-    yh[...], yl[...] = ys
-    for span in spans(y.shape[0], TILE):
-        xs = (high[CHIP, span, :], low[CHIP, span, :])
-        grads_out[CHIP, span, :] = grads[CHIP, span, :] + term(xs, ys, params)
-
-
-def near(params, y, high, low, grads):
-    rows, width = y.shape
-    return call(
-        near_kernel,
-        "near_pair",
-        (params, y, high, low, grads),
-        [VMEM] * 5,
-        [wide(2, rows, width)] + [thin(rows, width)] * 2,
-        [VMEM] * 3,
-        12 * rows * rows * width,
-        aliases={4: 0},
-    )
-
-
-def mate_kernel(ny, params, xh, xl, *refs):
-    received, outs, (yh, yl) = refs[:ny], refs[ny:-2], refs[-2:]
-    ys = halves(joined([y[...] for y in received], 0))
-    yh[...], yl[...] = ys
-    for start, out in zip(offsets([out.shape[0] for out in outs]), outs):
-        span = pl.ds(start, out.shape[0])
-        out[...] = term((xh[span, :], xl[span, :]), ys, params)
-
-
-def mate(params, xh, xl, ys):
-    rows, width = xh.shape
-    return call(
-        functools.partial(mate_kernel, len(ys)),
-        "mate_pair",
-        (params, xh, xl, *ys),
-        [VMEM] * (3 + len(ys)),
-        [wide(r, width) for r in RETURN] + [thin(rows, width)] * 2,
-        [VMEM] * (len(RETURN) + 2),
-        12 * rows * rows * width,
-    )
-
-
-def link_kernel(params, yh, yl, high, low, grads, grads_out):
+def both_kernel(first, params, x, *refs):
+    if first:
+        y, mate, high, low, yh, yl, *terms = refs
+        yh[...], yl[...] = halves(y[...])
+    else:
+        yh, yl, before, mate, high, low, *terms = refs
     ys = (yh[...], yl[...])
-    for span in spans(yh.shape[0], TILE):
-        xs = (high[LINK, span, :], low[LINK, span, :])
-        grads_out[LINK, span, :] = grads[LINK, span, :] + term(xs, ys, params)
-
-
-def link(params, ys, high, low, grads):
+    xs = halves(x[...])
+    high[...], low[...] = xs
+    coef = coefs(xs, ys, params)
+    start = 0
+    for term_out in terms:
+        rows = term_out.shape[0]
+        term_out[...] = weighted([c[start : start + rows] for c in coef], ys)
+        start += rows
+    part = dot3(coef, xs, ((0,), (0,)))
+    mate[...] = part if first else before[...] + part
+
+
+def both_terms(params, x, pieces, y=None, ys=(), before=None):
+    depth, width = x.shape
+    first = y is not None
+    inputs = (params, x, y) if first else (params, x, *ys, before)
+    rows = inputs[-1].shape[0]
+    outs = [wide(rows, width), thin(depth, width), thin(depth, width)]
+    outs += [thin(rows, width)] * 2 if first else []
+    outs += [wide(r, width) for r in pieces]
+    return call(
+        functools.partial(both_kernel, first),
+        "both_terms",
+        inputs,
+        [VMEM] * len(inputs),
+        outs,
+        [VMEM] * len(outs),
+        18 * rows * depth * width,
+        aliases={} if first else {4: 0},
+    )
+
+
+def add_kernel(side, pieces, params, *refs):
+    highs, lows, (high, low, grads, grads_out) = refs[:pieces], refs[pieces : 2 * pieces], refs[2 * pieces :]
+    ys = tuple(joined([y[...] for y in part], 0) if pieces > 1 else part[0][...] for part in (highs, lows))
+    for span in spans(grads.shape[1], TILE):
+        xs = (high[side, span, :], low[side, span, :])
+        grads_out[side, span, :] = grads[side, span, :] + term(xs, ys, params)
+
+
+def add_term(side, params, highs, lows, high, low, grads, hint=1):
     _, rows, width = grads.shape
-    return call(
-        link_kernel,
-        "link_pair",
-        (params, *ys, high, low, grads),
-        [VMEM] * 6,
+    pieces = len(highs)
+    last = 3 + 2 * pieces
+    return call(
+        functools.partial(add_kernel, side, pieces),
+        "add_term",
+        (params, *highs, *lows, high, low, grads),
+        [VMEM] * (last + 1),
         wide(2, rows, width),
         VMEM,
-        12 * rows * rows * width,
-        aliases={5: 0},
-    )
-
-
-def far_kernel(nr, params, y, *refs):
-    terms, (high, low, grads, grads_out, images_out, texts_out, result, sems) = refs[:nr], refs[nr:]
-    starts = offsets([piece.shape[0] for piece in terms])
-    for i, (start, piece) in enumerate(zip(starts, terms)):
-        span = pl.ds(start, piece.shape[0])
-        result[span, :] = grads[CHIP, span, :] + piece[...]
-        to_output(CHIP, result.at[span], images_out.at[span], texts_out.at[span], sems.at[i])
-    ys = halves(y[...])
-    for span in spans(grads.shape[1], TILE):
-        xs = (high[LINK, span, :], low[LINK, span, :])
-        grads_out[LINK, span, :] = grads[LINK, span, :] + term(xs, ys, params)
-    for i, (start, piece) in enumerate(zip(starts, terms)):
-        span = pl.ds(start, piece.shape[0])
-        pltpu.make_async_copy(result.at[span], images_out.at[span], sems.at[i]).wait()
-
-
-def far(params, y, terms, high, low, grads):
+        hint * 12 * rows * rows * width,
+        aliases={last: 0},
+    )
+
+
+def finish_kernel(side, start, term_in, grads, *refs):
+    images_out, texts_out, result, sem = refs[-4:]
+    span = pl.ds(start, term_in.shape[0])
+    result[...] = grads[side, span, :] + term_in[...]
+    to_output(side, result, images_out.at[span], texts_out.at[span], sem)
+    pltpu.make_async_copy(result, images_out.at[span], sem).wait()
+
+
+def finish(side, start, term_in, grads, outs=()):
     _, rows, width = grads.shape
-    first = 2 + len(terms) + 2
-    return call(
-        functools.partial(far_kernel, len(terms)),
-        "far_pair",
-        (params, y, *terms, high, low, grads),
-        [VMEM] * (first + 1),
-        [wide(2, rows, width)] + [wide(rows, width)] * 2,
-        [VMEM, ANY, ANY],
-        12 * rows * y.shape[0] * width,
-        [pltpu.VMEM((rows, width), F32), pltpu.SemaphoreType.DMA((len(terms),))],
-        {first: 0},
-    )
-
-
-def last_kernel(params, y, high, low, grads, images_in, texts_in, images_out, texts_out, result, sems):
-    yh, yl = halves(y[...])
-    depth, width = y.shape
-    xh, xl = high[LINK], low[LINK]
-    both = one_dot(xh, joined([yh, yl], 0), ((1,), (1,)))
-    total = both[:, :depth] + both[:, depth:] + one_dot(xl, yh, ((1,), (1,)))
-    scale, bias = params[0:1, 0:1], params[8:9, 0:1]
-    ch, cl = halves(scale * sigmoid(scale * total + bias))
-    cs = joined([ch, cl, ch], 1)
-    for i, start in enumerate(range(0, width, COLUMNS)):
-        span = pl.ds(start, COLUMNS)
-        yc = joined([yh[:, start : start + COLUMNS]] * 2 + [yl[:, start : start + COLUMNS]], 0)
-        result[:, span] = grads[LINK, :, span] + one_dot(cs, yc, ((1,), (0,)))
-        to_output(LINK, result.at[:, span], images_out.at[:, span], texts_out.at[:, span], sems.at[i])
-    for i, start in enumerate(range(0, width, COLUMNS)):
-        span = pl.ds(start, COLUMNS)
-        pltpu.make_async_copy(result.at[:, span], images_out.at[:, span], sems.at[i]).wait()
-
-
-def last(params, y, high, low, grads, outs):
-    _, rows, width = grads.shape
-    return call(
-        last_kernel,
-        "last_pair",
-        (params, y, high, low, grads, *outs),
-        [VMEM] * 5 + [ANY] * 2,
+    return call(
+        functools.partial(finish_kernel, side, start),
+        "finish",
+        (term_in, grads, *outs),
+        [VMEM] * 2 + [ANY] * len(outs),
         [wide(rows, width)] * 2,
         [ANY] * 2,
-        12 * rows * y.shape[0] * width,
-        [pltpu.VMEM((rows, width), F32), pltpu.SemaphoreType.DMA((width // COLUMNS,))],
-        {5: 0, 6: 1},
+        0,
+        [pltpu.VMEM(term_in.shape, F32), pltpu.SemaphoreType.DMA(())],
+        {2 + i: i for i in range(len(outs))},
     )
 
 
@@ -336,14 +290,20 @@
     a1 = [over_link(x) for x in a]
     b1 = on_chip(b)
     grads, high, low, params = own(a, b, scale, bias)
-    b1 = after(b1, grads)
-    a2 = [over_link(b1[s : s + r]) for s, r in zip(offsets(SECOND), SECOND)]
-    grads, bh, bl = near(params, b1, high, low, grads)
-    *terms, ah, al = mate(params, bh, bl, after(a1, grads))
-    terms = [on_chip(x) for x in terms]
-    grads = link(params, (ah, al), high, low, grads)
-    grads, *outs = far(params, after(a2[0], grads), terms, high, low, grads)
-    return tuple(last(params, after(a2[1], grads), high, low, grads, outs))
+    b1, head1 = after((b1, a1[0]), grads)
+    mate, ah, al, bh, bl, *terms = both_terms(params, head1, HEAD_TERMS, y=b1)
+    returned = [over_link(x) for x in terms]
+    grads = add_term(CHIP, params, [bh], [bl], high, low, grads)
+    mate, th, tl, *terms = both_terms(params, after(a1[1], grads), TAIL_TERMS, ys=(bh, bl), before=mate)
+    returned += [over_link(x) for x in terms]
+    mate = on_chip(mate)
+    grads = add_term(LINK, params, [after(ah, returned[0]), th], [al, tl], high, low, grads, HINT)
+    outs = finish(CHIP, 0, after(mate, grads), grads)
+    start = 0
+    for piece in returned:
+        outs = finish(LINK, start, after(piece, outs), grads, outs)
+        start += piece.shape[0]
+    return tuple(outs)
 
 
 def solution(mesh):

time: 65 us -> 65.8 us (1.012)
  waiting for transfers between devices: 6.59 us -> 9.21 us
  Pallas kernels: 32 us -> 31.1 us
  starting transfers between devices: 23.9 us -> 23.2 us
    ppermute x4 -> x5, waiting for transfers between devices: 6.58 us -> 9.21 us  [over_link(): lax.ppermute(x, 'dp', [(i, (i + 1) % peers if i % 2 else (i - 1) % peers)...]
    pallas_call x8 -> x11, Pallas kernels: 32 us -> 31.1 us  [call(): pl.pallas_call(kernel, out_shape=out_shape, in_specs=in_specs, out_specs=...]
    ppermute x4 -> x5, starting transfers between devices: 23.2 us -> 23.1 us  [over_link(): lax.ppermute(x, 'dp', [(i, (i + 1) % peers if i % 2 else (i - 1) % peers)...]
  transfers between devices with their start and end apart: 7 -> 7, of which waited for: 3 -> 2; matrix products, arithmetic and copies ran while one was open for 0% -> 0% of each run, Pallas kernels for 43% -> 44%
where the time goes in v3:
time: 65.8 us; the launch traced here: 65.6 us
  Pallas kernels  31.1 us (47%)
  starting transfers between devices  23.2 us (35%)
  waiting for transfers between devices  9.21 us (14%)
  between operations  2.19 us (3%)
    pallas_call x11, Pallas kernels, call(): pl.pallas_call(kernel, out_shape=out_shape, in_specs=in_specs, out_specs=...  31.1 us
    ppermute x5, starting transfers between devices, over_link(): lax.ppermute(x, 'dp', [(i, (i + 1) % peers if i % 2 else (i - 1) % peers)...  23.1 us
    ppermute x5, waiting for transfers between devices, over_link(): lax.ppermute(x, 'dp', [(i, (i + 1) % peers if i % 2 else (i - 1) % peers)...  9.21 us
  transfers between devices with their start and end apart: 7, of which 2 were waited for; matrix products, arithmetic and copies ran while one was open for 0% of the time, Pallas kernels for 44%

profile of v3, /device:TPU:0, one launch (start us, length us, event | category | flops | bytes accessed | tf_op | source)
XLA Modules:
  0.0 65.6 jit_solution(4896705927132588018)
XLA Ops:
  0.6 1.3 %pick.2.refs_0_ = f32[256,1152]{1,0:T(8,128)S(1)} custom-call(f32[512,1152]{1,0:T(8,128)} %images.3, f32[512,1152]{1,0:T(8,128)} %texts.3), custom_call_target="tpu_custom_call" | custom-call | bytes 4194304 | tf_op jit(solution)/shard_map/pick/pallas_call | solution.py:62
  1.9 8.3 %collective-permute-start.2 = (f32[256,1152]{1,0:T(8,128)S(1)}, f32[256,1152]{1,0:T(8,128)S(1)}, u32[]{:S(2)}, u32[]{:S(2)}) collective-permute-start(f32[256,1152]{1,0:T(8,128)S(1)} %pick.2.refs_0_), channel_id=1, source_target_pairs={{0,255},{1,2},{2,1},{3,4},{4,3},{5,6},{6,5},{7,8},{8,7},{9,10},{10... | collective-permute-start | bytes 3538952 | tf_op jit(solution)/shard_map/ppermute | solution.py:279
  10.2 2.0 %pick.3 = (f32[256,1152]{1,0:T(8,128)S(1)}, f32[512,1152]{1,0:T(8,128)S(1)}) custom-call(f32[512,1152]{1,0:T(8,128)} %images.3, f32[512,1152]{1,0:T(8,128)} %texts.3, f32[256,1152]{1,0:T(8,128)S(1)} %pick.2.refs_0_), custom_call_target="tpu_custom_call" | custom-call | bytes 4194304 | tf_op jit(solution)/shard_map/pick/pallas_call | solution.py:62
  12.3 0.1 collective-permute-start
  12.4 0.1 collective-permute-start.1
  13.8 6.7 %own_pair.1 = (f32[2,512,1152]{2,1,0:T(8,128)S(1)}, bf16[2,512,1152]{2,1,0:T(8,128)(2,1)S(1)}, bf16[2,512,1152]{2,1,0:T(8,128)(2,1)S(1)}, f32[16,128]{1,0:T(8,128)S(1)}) custom-call(f32[1,1]{1,0:T(1,128)} %bitcast.2.scale_ref, f32[1,1]{1,0:T(1,128)} %bitcast.3.bias_ref, f32[512,1152]{1,0:T(8,128)S(1)} %get-tuple-element.33.chip_block, ...), custom_call_target="tpu_custom_call" | custom-call | flops 54358179840 | bytes 4194304 | tf_op jit(solution)/shard_map/own_pair/pallas_call | solution.py:62
  20.4 3.7 %collective-permute-done.2.x = f32[256,1152]{1,0:T(8,128)S(1)} collective-permute-done((f32[256,1152]{1,0:T(8,128)S(1)}, f32[256,1152]{1,0:T(8,128)S(1)}, u32[]{:S(2)}, u32[]{:S(2)}) %collective-permute-start.2) | collective-permute-done | bytes 1179680 | tf_op jit(solution)/shard_map/ppermute | solution.py:279
  24.1 0.0 collective-permute-done.1.refs_0_
  24.1 3.5 %both_terms.2 = (f32[512,1152]{1,0:T(8,128)S(1)}, bf16[256,1152]{1,0:T(8,128)(2,1)S(1)}, bf16[256,1152]{1,0:T(8,128)(2,1)S(1)}, bf16[512,1152]{1,0:T(8,128)(2,1)...) custom-call(f32[16,128]{1,0:T(8,128)S(1)} %get-tuple-element.35.params, ...), custom_call_target="tpu_custom_call" | custom-call | flops 2717908992 | bytes 4194304 | tf_op jit(solution)/shard_map/both_terms/pallas_call | solution.py:62
  27.6 7.4 %collective-permute-start.5 = (f32[256,1152]{1,0:T(8,128)S(1)}, f32[256,1152]{1,0:T(8,128)S(1)}, u32[]{:S(2)}, u32[]{:S(2)}) collective-permute-start(f32[256,1152]{1,0:T(8,128)S(1)} %get-tuple-element.47), channel_id=1, source_target_pairs={{0,255},{1,2},{2,1},{3,4},{4,3},{5,6},{6,5},{7,8},{8,7},{9,10},{10... | collective-permute-start | bytes 3538952 | tf_op jit(solution)/shard_map/ppermute | solution.py:279
  35.0 4.6 %add_term.2.refs_6_ = f32[2,512,1152]{2,1,0:T(8,128)S(1)} custom-call(f32[16,128]{1,0:T(8,128)S(1)} %get-tuple-element.35.params, bf16[512,1152]{1,0:T(8,128)(2,1)S(1)} %get-tuple-element.39.refs_0_, bf16[512,1152]{1,0:T(8,128)(2,1)S(1)} %get-tuple-element.40.refs_1_, ...), custom_call_target="tpu_custom_call", output_to_operand_aliasing={{}: (5, {})} | custom-call | flops 3623878656 | bytes 4194304 | tf_op jit(solution)/shard_map/add_term/pallas_call | solution.py:62
  39.6 0.0 collective-permute-done.x
  39.6 3.8 %both_terms.3 = (f32[512,1152]{1,0:T(8,128)S(1)}, bf16[256,1152]{1,0:T(8,128)(2,1)S(1)}, bf16[256,1152]{1,0:T(8,128)(2,1)S(1)}, f32[112,1152]{1,0:T(8,128)S(1)}, f32[144,1152]{1,0:T(8,128)S(1)}) custom-call(f32[16,128]{1,0:T(8,128)S(1)} %get-tuple-element.35.params, f32[256,1152]{1,0:T(8,128)S(1)} %collective-permute-done.x, ...), custom_call_target="tpu_custom_call", output_to_operand_aliasing={{0}: (4, {})} | custom-call | flops 2717908992 | bytes 4194304 | tf_op jit(solution)/shard_map/both_terms/pallas_call | solution.py:62
  43.4 4.4 %collective-permute-start.4 = (f32[112,1152]{1,0:T(8,128)S(1)}, f32[112,1152]{1,0:T(8,128)S(1)}, u32[]{:S(2)}, u32[]{:S(2)}) collective-permute-start(f32[112,1152]{1,0:T(8,128)S(1)} %get-tuple-element.46), channel_id=1, source_target_pairs={{0,255},{1,2},{2,1},{3,4},{4,3},{5,6},{6,5},{7,8},{8,7},{9,10},{10... | collective-permute-start | bytes 1548296 | tf_op jit(solution)/shard_map/ppermute | solution.py:279
  47.8 2.9 %collective-permute-start.3 = (f32[144,1152]{1,0:T(8,128)S(1)}, f32[144,1152]{1,0:T(8,128)S(1)}, u32[]{:S(2)}, u32[]{:S(2)}) collective-permute-start(f32[144,1152]{1,0:T(8,128)S(1)} %get-tuple-element.45), channel_id=1, source_target_pairs={{0,255},{1,2},{2,1},{3,4},{4,3},{5,6},{6,5},{7,8},{8,7},{9,10},{10... | collective-permute-start | bytes 1990664 | tf_op jit(solution)/shard_map/ppermute | solution.py:279
  50.7 0.0 collective-permute-start.6
  50.7 0.0 collective-permute-done.5.term_in
  50.7 4.6 %add_term.3.grads = f32[2,512,1152]{2,1,0:T(8,128)S(1)} custom-call(f32[16,128]{1,0:T(8,128)S(1)} %get-tuple-element.35.params, bf16[256,1152]{1,0:T(8,128)(2,1)S(1)} %get-tuple-element.50.refs_0_, bf16[256,1152]{1,0:T(8,128)(2,1)S(1)} %get-tuple-element.51.refs_1_, bf16[256,1152]{1,0:T(8,128)(2,1)S(1)} %get-tuple-element.52.refs_2_, ...), custom_call_target="tpu_custom_call", output_to_operand_aliasing={{}: (7, {})} | custom-call | flops 36238786560 | bytes 4194304 | tf_op jit(solution)/shard_map/add_term/pallas_call | solution.py:62
  55.3 0.0 collective-permute-done.6.term_in
  55.3 1.7 %finish.4 = (f32[512,1152]{1,0:T(8,128)}, f32[512,1152]{1,0:T(8,128)}) custom-call(f32[512,1152]{1,0:T(8,128)S(1)} %collective-permute-done.6.term_in, f32[2,512,1152]{2,1,0:T(8,128)S(1)} %add_term.3.grads), custom_call_target="tpu_custom_call" | custom-call | bytes 4194304 | tf_op jit(solution)/shard_map/finish/pallas_call | solution.py:62
  57.0 1.1 %finish.5 = (f32[512,1152]{1,0:T(8,128)}, f32[512,1152]{1,0:T(8,128)}) custom-call(f32[256,1152]{1,0:T(8,128)S(1)} %collective-permute-done.5.term_in, f32[2,512,1152]{2,1,0:T(8,128)S(1)} %add_term.3.grads, f32[512,1152]{1,0:T(8,128)} %get-tuple-element.55.refs_0_, f32[512,1152]{1,0:T(8,128)} %get-tuple-element.56.refs_1_), custom_call_target="tpu_custom_call", output_to_operand_aliasing={{0}: (2, {}), {1}: (3, {})} | custom-call | bytes 4194304 | tf_op jit(solution)/shard_map/finish/pallas_call | solution.py:62
  58.2 0.0 collective-permute-done.4.term_in
  58.2 0.9 %finish.6 = (f32[512,1152]{1,0:T(8,128)}, f32[512,1152]{1,0:T(8,128)}) custom-call(f32[112,1152]{1,0:T(8,128)S(1)} %collective-permute-done.4.term_in, f32[2,512,1152]{2,1,0:T(8,128)S(1)} %add_term.3.grads, f32[512,1152]{1,0:T(8,128)} %get-tuple-element.58.refs_0_, f32[512,1152]{1,0:T(8,128)} %get-tuple-element.59.refs_1_), custom_call_target="tpu_custom_call", output_to_operand_aliasing={{0}: (2, {}), {1}: (3, {})} | custom-call | bytes 4194304 | tf_op jit(solution)/shard_map/finish/pallas_call | solution.py:62
  59.0 5.5 %collective-permute-done.3.term_in = f32[144,1152]{1,0:T(8,128)S(1)} collective-permute-done((f32[144,1152]{1,0:T(8,128)S(1)}, f32[144,1152]{1,0:T(8,128)S(1)}, u32[]{:S(2)}, u32[]{:S(2)}) %collective-permute-start.3) | collective-permute-done | bytes 663584 | tf_op jit(solution)/shard_map/ppermute | solution.py:279
  64.6 0.9 %finish.7 = (f32[512,1152]{1,0:T(8,128)}, f32[512,1152]{1,0:T(8,128)}) custom-call(f32[144,1152]{1,0:T(8,128)S(1)} %collective-permute-done.3.term_in, f32[2,512,1152]{2,1,0:T(8,128)S(1)} %add_term.3.grads, f32[512,1152]{1,0:T(8,128)} %get-tuple-element.61.refs_0_, f32[512,1152]{1,0:T(8,128)} %get-tuple-element.62.refs_1_), custom_call_target="tpu_custom_call", output_to_operand_aliasing={{0}: (2, {}), {1}: (3, {})} | custom-call | bytes 4194304 | tf_op jit(solution)/shard_map/finish/pallas_call | solution.py:62
Async XLA Ops:
  1.9 22.2 %collective-permute-start.2 = (f32[256,1152]{1,0:T(8,128)S(1)}, f32[256,1152]{1,0:T(8,128)S(1)}, u32[]{:S(2)}, u32[]{:S(2)}) collective-permute-start(f32[256,1152]{1,0:T(8,128)S(1)} %pick.2.refs_0_), channel_id=1, source_target_pairs={{0,255},{1,2},{2,1},{3,4},{4,3},{5,6},{6,5},{7,8},{8,7},{9,10},{10... | collective-permute-start | bytes 3538952 | tf_op jit(solution)/shard_map/ppermute | solution.py:279
  12.3 27.3 %collective-permute-start = (f32[256,1152]{1,0:T(8,128)S(1)}, f32[256,1152]{1,0:T(8,128)S(1)}, u32[]{:S(2)}, u32[]{:S(2)}) collective-permute-start(f32[256,1152]{1,0:T(8,128)S(1)} %get-tuple-element.34.refs_1_), channel_id=1, source_target_pairs={{0,255},{1,2},{2,1},{3,4},{4,3},{5,6},{6,5},{7,8},{8,7},{9,10},{10... | collective-permute-start | bytes 3538952 | tf_op jit(solution)/shard_map/ppermute | solution.py:279
  12.4 11.7 %collective-permute-start.1 = (f32[512,1152]{1,0:T(8,128)S(1)}, f32[512,1152]{1,0:T(8,128)S(1)}, u32[]{:S(2)}, u32[]{:S(2)}) collective-permute-start(f32[512,1152]{1,0:T(8,128)S(1)} %get-tuple-element.33.chip_block), channel_id=1, source_target_pairs={{0,1},{1,0},{2,3},{3,2},{4,5},{5,4},{6,7},{7,6},{8,9},{9,8},{10,11... | collective-permute-start | bytes 7077896 | tf_op jit(solution)/shard_map/ppermute | solution.py:284
  27.6 23.1 %collective-permute-start.5 = (f32[256,1152]{1,0:T(8,128)S(1)}, f32[256,1152]{1,0:T(8,128)S(1)}, u32[]{:S(2)}, u32[]{:S(2)}) collective-permute-start(f32[256,1152]{1,0:T(8,128)S(1)} %get-tuple-element.47), channel_id=1, source_target_pairs={{0,255},{1,2},{2,1},{3,4},{4,3},{5,6},{6,5},{7,8},{8,7},{9,10},{10... | collective-permute-start | bytes 3538952 | tf_op jit(solution)/shard_map/ppermute | solution.py:279
  43.4 14.7 %collective-permute-start.4 = (f32[112,1152]{1,0:T(8,128)S(1)}, f32[112,1152]{1,0:T(8,128)S(1)}, u32[]{:S(2)}, u32[]{:S(2)}) collective-permute-start(f32[112,1152]{1,0:T(8,128)S(1)} %get-tuple-element.46), channel_id=1, source_target_pairs={{0,255},{1,2},{2,1},{3,4},{4,3},{5,6},{6,5},{7,8},{8,7},{9,10},{10... | collective-permute-start | bytes 1548296 | tf_op jit(solution)/shard_map/ppermute | solution.py:279
  47.8 16.8 %collective-permute-start.3 = (f32[144,1152]{1,0:T(8,128)S(1)}, f32[144,1152]{1,0:T(8,128)S(1)}, u32[]{:S(2)}, u32[]{:S(2)}) collective-permute-start(f32[144,1152]{1,0:T(8,128)S(1)} %get-tuple-element.45), channel_id=1, source_target_pairs={{0,255},{1,2},{2,1},{3,4},{4,3},{5,6},{6,5},{7,8},{8,7},{9,10},{10... | collective-permute-start | bytes 1990664 | tf_op jit(solution)/shard_map/ppermute | solution.py:279
  50.7 4.6 %collective-permute-start.6 = (f32[512,1152]{1,0:T(8,128)S(1)}, f32[512,1152]{1,0:T(8,128)S(1)}, u32[]{:S(2)}, u32[]{:S(2)}) collective-permute-start(f32[512,1152]{1,0:T(8,128)S(1)} %get-tuple-element.48), channel_id=1, source_target_pairs={{0,1},{1,0},{2,3},{3,2},{4,5},{5,4},{6,7},{7,6},{8,9},{9,8},{10,11... | collective-permute-start | bytes 7077896 | tf_op jit(solution)/shard_map/ppermute | solution.py:284

commit v4 on v3

--- a/solution.py
+++ b/solution.py
@@ -182,12 +182,8 @@
     )
 
 
-def both_kernel(first, params, x, *refs):
-    if first:
-        y, mate, high, low, yh, yl, *terms = refs
-        yh[...], yl[...] = halves(y[...])
-    else:
-        yh, yl, before, mate, high, low, *terms = refs
+def both_kernel(first, params, x, yh, yl, *refs):
+    before, (mate, high, low, *terms) = (None, refs) if first else (refs[0], refs[1:])
     ys = (yh[...], yl[...])
     xs = halves(x[...])
     high[...], low[...] = xs
@@ -201,13 +197,12 @@
     mate[...] = part if first else before[...] + part
 
 
-def both_terms(params, x, pieces, y=None, ys=(), before=None):
+def both_terms(params, x, pieces, ys, before=None):
     depth, width = x.shape
-    first = y is not None
-    inputs = (params, x, y) if first else (params, x, *ys, before)
-    rows = inputs[-1].shape[0]
+    rows = ys[0].shape[0]
+    first = before is None
+    inputs = (params, x, *ys) if first else (params, x, *ys, before)
     outs = [wide(rows, width), thin(depth, width), thin(depth, width)]
-    outs += [thin(rows, width)] * 2 if first else []
     outs += [wide(r, width) for r in pieces]
     return call(
         functools.partial(both_kernel, first),
@@ -218,6 +213,28 @@
         [VMEM] * len(outs),
         18 * rows * depth * width,
         aliases={} if first else {4: 0},
+    )
+
+
+def near_kernel(params, y, high, low, grads, grads_out, yh, yl):
+    ys = halves(y[...])
+    yh[...], yl[...] = ys
+    for span in spans(y.shape[0], TILE):
+        xs = (high[CHIP, span, :], low[CHIP, span, :])
+        grads_out[CHIP, span, :] = grads[CHIP, span, :] + term(xs, ys, params)
+
+
+def near(params, y, high, low, grads):
+    rows, width = y.shape
+    return call(
+        near_kernel,
+        "near_pair",
+        (params, y, high, low, grads),
+        [VMEM] * 5,
+        [wide(2, rows, width)] + [thin(rows, width)] * 2,
+        [VMEM] * 3,
+        12 * rows * rows * width,
+        aliases={4: 0},
     )
 
 
@@ -290,11 +307,10 @@
     a1 = [over_link(x) for x in a]
     b1 = on_chip(b)
     grads, high, low, params = own(a, b, scale, bias)
-    b1, head1 = after((b1, a1[0]), grads)
-    mate, ah, al, bh, bl, *terms = both_terms(params, head1, HEAD_TERMS, y=b1)
+    grads, *ys = near(params, after(b1, grads), high, low, grads)
+    mate, ah, al, *terms = both_terms(params, after(a1[0], grads), HEAD_TERMS, ys)
     returned = [over_link(x) for x in terms]
-    grads = add_term(CHIP, params, [bh], [bl], high, low, grads)
-    mate, th, tl, *terms = both_terms(params, after(a1[1], grads), TAIL_TERMS, ys=(bh, bl), before=mate)
+    mate, th, tl, *terms = both_terms(params, after(a1[1], mate), TAIL_TERMS, ys, mate)
     returned += [over_link(x) for x in terms]
     mate = on_chip(mate)
     grads = add_term(LINK, params, [after(ah, returned[0]), th], [al, tl], high, low, grads, HINT)

time: 65.8 us -> 64.6 us (0.982)
  waiting for transfers between devices: 9.21 us -> 7.95 us
    ppermute x5, waiting for transfers between devices: 9.21 us -> 7.94 us  [over_link(): lax.ppermute(x, 'dp', [(i, (i + 1) % peers if i % 2 else (i - 1) % peers)...]
  transfers between devices with their start and end apart: 7 -> 7, of which waited for: 2 -> 3; matrix products, arithmetic and copies ran while one was open for 0% -> 0% of each run, Pallas kernels for 44% -> 45%
where the time goes in v4:
time: 64.6 us; the launch traced here: 64.4 us
  Pallas kernels  31.1 us (48%)
  starting transfers between devices  23.2 us (36%)
  waiting for transfers between devices  7.95 us (12%)
  between operations  2.2 us (3%)
    pallas_call x11, Pallas kernels, call(): pl.pallas_call(kernel, out_shape=out_shape, in_specs=in_specs, out_specs=...  31.1 us
    ppermute x5, starting transfers between devices, over_link(): lax.ppermute(x, 'dp', [(i, (i + 1) % peers if i % 2 else (i - 1) % peers)...  23.1 us
    ppermute x5, waiting for transfers between devices, over_link(): lax.ppermute(x, 'dp', [(i, (i + 1) % peers if i % 2 else (i - 1) % peers)...  7.94 us
  transfers between devices with their start and end apart: 7, of which 3 were waited for; matrix products, arithmetic and copies ran while one was open for 0% of the time, Pallas kernels for 45%

profile of v4, /device:TPU:0, one launch (start us, length us, event | category | flops | bytes accessed | tf_op | source)
XLA Modules:
  0.0 64.4 jit_solution(4241402703680049786)
XLA Ops:
  0.6 1.3 %pick.2.refs_0_ = f32[256,1152]{1,0:T(8,128)S(1)} custom-call(f32[512,1152]{1,0:T(8,128)} %images.3, f32[512,1152]{1,0:T(8,128)} %texts.3), custom_call_target="tpu_custom_call" | custom-call | bytes 4194304 | tf_op jit(solution)/shard_map/pick/pallas_call | solution.py:62
  1.9 8.3 %collective-permute-start.1 = (f32[256,1152]{1,0:T(8,128)S(1)}, f32[256,1152]{1,0:T(8,128)S(1)}, u32[]{:S(2)}, u32[]{:S(2)}) collective-permute-start(f32[256,1152]{1,0:T(8,128)S(1)} %pick.2.refs_0_), channel_id=1, source_target_pairs={{0,255},{1,2},{2,1},{3,4},{4,3},{5,6},{6,5},{7,8},{8,7},{9,10},{10... | collective-permute-start | bytes 3538952 | tf_op jit(solution)/shard_map/ppermute | solution.py:296
  10.2 2.0 %pick.3 = (f32[256,1152]{1,0:T(8,128)S(1)}, f32[512,1152]{1,0:T(8,128)S(1)}) custom-call(f32[512,1152]{1,0:T(8,128)} %images.3, f32[512,1152]{1,0:T(8,128)} %texts.3, f32[256,1152]{1,0:T(8,128)S(1)} %pick.2.refs_0_), custom_call_target="tpu_custom_call" | custom-call | bytes 4194304 | tf_op jit(solution)/shard_map/pick/pallas_call | solution.py:62
  12.3 0.1 collective-permute-start
  12.4 0.1 collective-permute-start.2
  13.8 6.7 %own_pair.1 = (f32[2,512,1152]{2,1,0:T(8,128)S(1)}, bf16[2,512,1152]{2,1,0:T(8,128)(2,1)S(1)}, bf16[2,512,1152]{2,1,0:T(8,128)(2,1)S(1)}, f32[16,128]{1,0:T(8,128)S(1)}) custom-call(f32[1,1]{1,0:T(1,128)} %bitcast.2.scale_ref, f32[1,1]{1,0:T(1,128)} %bitcast.3.bias_ref, f32[512,1152]{1,0:T(8,128)S(1)} %get-tuple-element.34.chip_block, ...), custom_call_target="tpu_custom_call" | custom-call | flops 54358179840 | bytes 4194304 | tf_op jit(solution)/shard_map/own_pair/pallas_call | solution.py:62
  20.5 0.0 collective-permute-done.2.y
  20.5 4.6 %near_pair.1 = (f32[2,512,1152]{2,1,0:T(8,128)S(1)}, bf16[512,1152]{1,0:T(8,128)(2,1)S(1)}, bf16[512,1152]{1,0:T(8,128)(2,1)S(1)}) custom-call(f32[16,128]{1,0:T(8,128)S(1)} %get-tuple-element.36.params, f32[512,1152]{1,0:T(8,128)S(1)} %collective-permute-done.2.y, ...), custom_call_target="tpu_custom_call", output_to_operand_aliasing={{0}: (4, {})} | custom-call | flops 3623878656 | bytes 4194304 | tf_op jit(solution)/shard_map/near_pair/pallas_call | solution.py:62
  25.2 0.0 collective-permute-done.1.x
  25.2 3.4 %both_terms.2 = (f32[512,1152]{1,0:T(8,128)S(1)}, bf16[256,1152]{1,0:T(8,128)(2,1)S(1)}, bf16[256,1152]{1,0:T(8,128)(2,1)S(1)}, f32[256,1152]{1,0:T(8,128)S(1)}) custom-call(f32[16,128]{1,0:T(8,128)S(1)} %get-tuple-element.36.params, f32[256,1152]{1,0:T(8,128)S(1)} %collective-permute-done.1.x, bf16[512,1152]{1,0:T(8,128)(2,1)S(1)} %get-tuple-element.43.yh, ...), custom_call_target="tpu_custom_call" | custom-call | flops 2717908992 | bytes 4194304 | tf_op jit(solution)/shard_map/both_terms/pallas_call | solution.py:62
  28.6 7.3 %collective-permute-start.5 = (f32[256,1152]{1,0:T(8,128)S(1)}, f32[256,1152]{1,0:T(8,128)S(1)}, u32[]{:S(2)}, u32[]{:S(2)}) collective-permute-start(f32[256,1152]{1,0:T(8,128)S(1)} %get-tuple-element.49), channel_id=1, source_target_pairs={{0,255},{1,2},{2,1},{3,4},{4,3},{5,6},{6,5},{7,8},{8,7},{9,10},{10... | collective-permute-start | bytes 3538952 | tf_op jit(solution)/shard_map/ppermute | solution.py:296
  36.0 0.8 %collective-permute-done.x = f32[256,1152]{1,0:T(8,128)S(1)} collective-permute-done((f32[256,1152]{1,0:T(8,128)S(1)}, f32[256,1152]{1,0:T(8,128)S(1)}, u32[]{:S(2)}, u32[]{:S(2)}) %collective-permute-start) | collective-permute-done | bytes 1179680 | tf_op jit(solution)/shard_map/ppermute | solution.py:296
  36.7 3.8 %both_terms.3 = (f32[512,1152]{1,0:T(8,128)S(1)}, bf16[256,1152]{1,0:T(8,128)(2,1)S(1)}, bf16[256,1152]{1,0:T(8,128)(2,1)S(1)}, f32[112,1152]{1,0:T(8,128)S(1)}, f32[144,1152]{1,0:T(8,128)S(1)}) custom-call(f32[16,128]{1,0:T(8,128)S(1)} %get-tuple-element.36.params, f32[256,1152]{1,0:T(8,128)S(1)} %collective-permute-done.x, ...), custom_call_target="tpu_custom_call", output_to_operand_aliasing={{0}: (4, {})} | custom-call | flops 2717908992 | bytes 4194304 | tf_op jit(solution)/shard_map/both_terms/pallas_call | solution.py:62
  40.5 7.3 %collective-permute-start.4 = (f32[112,1152]{1,0:T(8,128)S(1)}, f32[112,1152]{1,0:T(8,128)S(1)}, u32[]{:S(2)}, u32[]{:S(2)}) collective-permute-start(f32[112,1152]{1,0:T(8,128)S(1)} %get-tuple-element.48), channel_id=1, source_target_pairs={{0,255},{1,2},{2,1},{3,4},{4,3},{5,6},{6,5},{7,8},{8,7},{9,10},{10... | collective-permute-start | bytes 1548296 | tf_op jit(solution)/shard_map/ppermute | solution.py:296
  47.8 0.1 collective-permute-start.3
  47.9 0.0 collective-permute-start.6
  47.9 2.1 %collective-permute-done.5.term_in = f32[256,1152]{1,0:T(8,128)S(1)} collective-permute-done((f32[256,1152]{1,0:T(8,128)S(1)}, f32[256,1152]{1,0:T(8,128)S(1)}, u32[]{:S(2)}, u32[]{:S(2)}) %collective-permute-start.5) | collective-permute-done | bytes 1179680 | tf_op jit(solution)/shard_map/ppermute | solution.py:296
  50.0 4.6 %add_term.1.grads = f32[2,512,1152]{2,1,0:T(8,128)S(1)} custom-call(f32[16,128]{1,0:T(8,128)S(1)} %get-tuple-element.36.params, bf16[256,1152]{1,0:T(8,128)(2,1)S(1)} %get-tuple-element.52.refs_0_, bf16[256,1152]{1,0:T(8,128)(2,1)S(1)} %get-tuple-element.53.refs_1_, bf16[256,1152]{1,0:T(8,128)(2,1)S(1)} %get-tuple-element.54.refs_2_, ...), custom_call_target="tpu_custom_call", output_to_operand_aliasing={{}: (7, {})} | custom-call | flops 36238786560 | bytes 4194304 | tf_op jit(solution)/shard_map/add_term/pallas_call | solution.py:62
  54.5 0.0 collective-permute-done.6.term_in
  54.5 1.7 %finish.4 = (f32[512,1152]{1,0:T(8,128)}, f32[512,1152]{1,0:T(8,128)}) custom-call(f32[512,1152]{1,0:T(8,128)S(1)} %collective-permute-done.6.term_in, f32[2,512,1152]{2,1,0:T(8,128)S(1)} %add_term.1.grads), custom_call_target="tpu_custom_call" | custom-call | bytes 4194304 | tf_op jit(solution)/shard_map/finish/pallas_call | solution.py:62
  56.2 1.1 %finish.5 = (f32[512,1152]{1,0:T(8,128)}, f32[512,1152]{1,0:T(8,128)}) custom-call(f32[256,1152]{1,0:T(8,128)S(1)} %collective-permute-done.5.term_in, f32[2,512,1152]{2,1,0:T(8,128)S(1)} %add_term.1.grads, f32[512,1152]{1,0:T(8,128)} %get-tuple-element.57.refs_0_, f32[512,1152]{1,0:T(8,128)} %get-tuple-element.58.refs_1_), custom_call_target="tpu_custom_call", output_to_operand_aliasing={{0}: (2, {}), {1}: (3, {})} | custom-call | bytes 4194304 | tf_op jit(solution)/shard_map/finish/pallas_call | solution.py:62
  57.3 0.0 collective-permute-done.4.term_in
  57.4 0.9 %finish.6 = (f32[512,1152]{1,0:T(8,128)}, f32[512,1152]{1,0:T(8,128)}) custom-call(f32[112,1152]{1,0:T(8,128)S(1)} %collective-permute-done.4.term_in, f32[2,512,1152]{2,1,0:T(8,128)S(1)} %add_term.1.grads, f32[512,1152]{1,0:T(8,128)} %get-tuple-element.60.refs_0_, f32[512,1152]{1,0:T(8,128)} %get-tuple-element.61.refs_1_), custom_call_target="tpu_custom_call", output_to_operand_aliasing={{0}: (2, {}), {1}: (3, {})} | custom-call | bytes 4194304 | tf_op jit(solution)/shard_map/finish/pallas_call | solution.py:62
  58.2 5.1 %collective-permute-done.3.term_in = f32[144,1152]{1,0:T(8,128)S(1)} collective-permute-done((f32[144,1152]{1,0:T(8,128)S(1)}, f32[144,1152]{1,0:T(8,128)S(1)}, u32[]{:S(2)}, u32[]{:S(2)}) %collective-permute-start.3) | collective-permute-done | bytes 663584 | tf_op jit(solution)/shard_map/ppermute | solution.py:296
  63.3 1.0 %finish.7 = (f32[512,1152]{1,0:T(8,128)}, f32[512,1152]{1,0:T(8,128)}) custom-call(f32[144,1152]{1,0:T(8,128)S(1)} %collective-permute-done.3.term_in, f32[2,512,1152]{2,1,0:T(8,128)S(1)} %add_term.1.grads, f32[512,1152]{1,0:T(8,128)} %get-tuple-element.63.refs_0_, f32[512,1152]{1,0:T(8,128)} %get-tuple-element.64.refs_1_), custom_call_target="tpu_custom_call", output_to_operand_aliasing={{0}: (2, {}), {1}: (3, {})} | custom-call | bytes 4194304 | tf_op jit(solution)/shard_map/finish/pallas_call | solution.py:62
Async XLA Ops:
  1.9 23.3 %collective-permute-start.1 = (f32[256,1152]{1,0:T(8,128)S(1)}, f32[256,1152]{1,0:T(8,128)S(1)}, u32[]{:S(2)}, u32[]{:S(2)}) collective-permute-start(f32[256,1152]{1,0:T(8,128)S(1)} %pick.2.refs_0_), channel_id=1, source_target_pairs={{0,255},{1,2},{2,1},{3,4},{4,3},{5,6},{6,5},{7,8},{8,7},{9,10},{10... | collective-permute-start | bytes 3538952 | tf_op jit(solution)/shard_map/ppermute | solution.py:296
  12.3 24.5 %collective-permute-start = (f32[256,1152]{1,0:T(8,128)S(1)}, f32[256,1152]{1,0:T(8,128)S(1)}, u32[]{:S(2)}, u32[]{:S(2)}) collective-permute-start(f32[256,1152]{1,0:T(8,128)S(1)} %get-tuple-element.35.refs_1_), channel_id=1, source_target_pairs={{0,255},{1,2},{2,1},{3,4},{4,3},{5,6},{6,5},{7,8},{8,7},{9,10},{10... | collective-permute-start | bytes 3538952 | tf_op jit(solution)/shard_map/ppermute | solution.py:296
  12.4 8.1 %collective-permute-start.2 = (f32[512,1152]{1,0:T(8,128)S(1)}, f32[512,1152]{1,0:T(8,128)S(1)}, u32[]{:S(2)}, u32[]{:S(2)}) collective-permute-start(f32[512,1152]{1,0:T(8,128)S(1)} %get-tuple-element.34.chip_block), channel_id=1, source_target_pairs={{0,1},{1,0},{2,3},{3,2},{4,5},{5,4},{6,7},{7,6},{8,9},{9,8},{10,11... | collective-permute-start | bytes 7077896 | tf_op jit(solution)/shard_map/ppermute | solution.py:301
  28.6 21.3 %collective-permute-start.5 = (f32[256,1152]{1,0:T(8,128)S(1)}, f32[256,1152]{1,0:T(8,128)S(1)}, u32[]{:S(2)}, u32[]{:S(2)}) collective-permute-start(f32[256,1152]{1,0:T(8,128)S(1)} %get-tuple-element.49), channel_id=1, source_target_pairs={{0,255},{1,2},{2,1},{3,4},{4,3},{5,6},{6,5},{7,8},{8,7},{9,10},{10... | collective-permute-start | bytes 3538952 | tf_op jit(solution)/shard_map/ppermute | solution.py:296
  40.5 16.8 %collective-permute-start.4 = (f32[112,1152]{1,0:T(8,128)S(1)}, f32[112,1152]{1,0:T(8,128)S(1)}, u32[]{:S(2)}, u32[]{:S(2)}) collective-permute-start(f32[112,1152]{1,0:T(8,128)S(1)} %get-tuple-element.48), channel_id=1, source_target_pairs={{0,255},{1,2},{2,1},{3,4},{4,3},{5,6},{6,5},{7,8},{8,7},{9,10},{10... | collective-permute-start | bytes 1548296 | tf_op jit(solution)/shard_map/ppermute | solution.py:296
  47.8 15.5 %collective-permute-start.3 = (f32[144,1152]{1,0:T(8,128)S(1)}, f32[144,1152]{1,0:T(8,128)S(1)}, u32[]{:S(2)}, u32[]{:S(2)}) collective-permute-start(f32[144,1152]{1,0:T(8,128)S(1)} %get-tuple-element.47), channel_id=1, source_target_pairs={{0,255},{1,2},{2,1},{3,4},{4,3},{5,6},{6,5},{7,8},{8,7},{9,10},{10... | collective-permute-start | bytes 1990664 | tf_op jit(solution)/shard_map/ppermute | solution.py:296
  47.9 6.7 %collective-permute-start.6 = (f32[512,1152]{1,0:T(8,128)S(1)}, f32[512,1152]{1,0:T(8,128)S(1)}, u32[]{:S(2)}, u32[]{:S(2)}) collective-permute-start(f32[512,1152]{1,0:T(8,128)S(1)} %get-tuple-element.50), channel_id=1, source_target_pairs={{0,1},{1,0},{2,3},{3,2},{4,5},{5,4},{6,7},{7,6},{8,9},{9,8},{10,11... | collective-permute-start | bytes 7077896 | tf_op jit(solution)/shard_map/ppermute | solution.py:301

commit v5 on v4

--- a/solution.py
+++ b/solution.py
@@ -18,7 +18,7 @@
 
 HEAD = 256
 HEAD_TERMS = (256,)
-TAIL_TERMS = (112, 144)
+TAIL_TERMS = (256,)
 TILE = 256
 
 

time: 64.6 us -> 64.1 us (level)
  Pallas kernels: 31.1 us -> 30.2 us
    pallas_call x11 -> x10, Pallas kernels: 31.1 us -> 30.2 us  [call(): pl.pallas_call(kernel, out_shape=out_shape, in_specs=in_specs, out_specs=...]
    ppermute x5 -> x4, waiting for transfers between devices: 7.94 us -> 8.46 us  [over_link(): lax.ppermute(x, 'dp', [(i, (i + 1) % peers if i % 2 else (i - 1) % peers)...]
    ppermute x5 -> x4, starting transfers between devices: 23.1 us -> 23 us  [over_link(): lax.ppermute(x, 'dp', [(i, (i + 1) % peers if i % 2 else (i - 1) % peers)...]
  transfers between devices with their start and end apart: 7 -> 6, of which waited for: 3 -> 3; matrix products, arithmetic and copies ran while one was open for 0% -> 0% of each run, Pallas kernels for 45% -> 43%
where the time goes in v5:
time: 64.1 us; the launch traced here: 63.9 us
  Pallas kernels  30.2 us (47%)
  starting transfers between devices  23.1 us (36%)
  waiting for transfers between devices  8.46 us (13%)
  between operations  2.18 us (3%)
    pallas_call x10, Pallas kernels, call(): pl.pallas_call(kernel, out_shape=out_shape, in_specs=in_specs, out_specs=...  30.2 us
    ppermute x4, starting transfers between devices, over_link(): lax.ppermute(x, 'dp', [(i, (i + 1) % peers if i % 2 else (i - 1) % peers)...  23 us
    ppermute x4, waiting for transfers between devices, over_link(): lax.ppermute(x, 'dp', [(i, (i + 1) % peers if i % 2 else (i - 1) % peers)...  8.46 us
  transfers between devices with their start and end apart: 6, of which 3 were waited for; matrix products, arithmetic and copies ran while one was open for 0% of the time, Pallas kernels for 43%

profile of v5, /device:TPU:0, one launch (start us, length us, event | category | flops | bytes accessed | tf_op | source)
XLA Modules:
  0.0 63.9 jit_solution(9666221787359280671)
XLA Ops:
  0.6 1.3 %pick.2.refs_0_ = f32[256,1152]{1,0:T(8,128)S(1)} custom-call(f32[512,1152]{1,0:T(8,128)} %images.3, f32[512,1152]{1,0:T(8,128)} %texts.3), custom_call_target="tpu_custom_call" | custom-call | bytes 4194304 | tf_op jit(solution)/shard_map/pick/pallas_call | solution.py:62
  1.9 8.3 %collective-permute-start.1 = (f32[256,1152]{1,0:T(8,128)S(1)}, f32[256,1152]{1,0:T(8,128)S(1)}, u32[]{:S(2)}, u32[]{:S(2)}) collective-permute-start(f32[256,1152]{1,0:T(8,128)S(1)} %pick.2.refs_0_), channel_id=1, source_target_pairs={{0,255},{1,2},{2,1},{3,4},{4,3},{5,6},{6,5},{7,8},{8,7},{9,10},{10... | collective-permute-start | bytes 3538952 | tf_op jit(solution)/shard_map/ppermute | solution.py:296
  10.2 2.0 %pick.3 = (f32[256,1152]{1,0:T(8,128)S(1)}, f32[512,1152]{1,0:T(8,128)S(1)}) custom-call(f32[512,1152]{1,0:T(8,128)} %images.3, f32[512,1152]{1,0:T(8,128)} %texts.3, f32[256,1152]{1,0:T(8,128)S(1)} %pick.2.refs_0_), custom_call_target="tpu_custom_call" | custom-call | bytes 4194304 | tf_op jit(solution)/shard_map/pick/pallas_call | solution.py:62
  12.3 0.1 collective-permute-start
  12.4 0.1 collective-permute-start.2
  13.8 6.7 %own_pair.1 = (f32[2,512,1152]{2,1,0:T(8,128)S(1)}, bf16[2,512,1152]{2,1,0:T(8,128)(2,1)S(1)}, bf16[2,512,1152]{2,1,0:T(8,128)(2,1)S(1)}, f32[16,128]{1,0:T(8,128)S(1)}) custom-call(f32[1,1]{1,0:T(1,128)} %bitcast.2.scale_ref, f32[1,1]{1,0:T(1,128)} %bitcast.3.bias_ref, f32[512,1152]{1,0:T(8,128)S(1)} %get-tuple-element.30.chip_block, ...), custom_call_target="tpu_custom_call" | custom-call | flops 54358179840 | bytes 4194304 | tf_op jit(solution)/shard_map/own_pair/pallas_call | solution.py:62
  20.5 0.0 collective-permute-done.2.y
  20.5 4.6 %near_pair.1 = (f32[2,512,1152]{2,1,0:T(8,128)S(1)}, bf16[512,1152]{1,0:T(8,128)(2,1)S(1)}, bf16[512,1152]{1,0:T(8,128)(2,1)S(1)}) custom-call(f32[16,128]{1,0:T(8,128)S(1)} %get-tuple-element.32.params, f32[512,1152]{1,0:T(8,128)S(1)} %collective-permute-done.2.y, ...), custom_call_target="tpu_custom_call", output_to_operand_aliasing={{0}: (4, {})} | custom-call | flops 3623878656 | bytes 4194304 | tf_op jit(solution)/shard_map/near_pair/pallas_call | solution.py:62
  25.2 0.0 collective-permute-done.1.x
  25.2 3.4 %both_terms.2 = (f32[512,1152]{1,0:T(8,128)S(1)}, bf16[256,1152]{1,0:T(8,128)(2,1)S(1)}, bf16[256,1152]{1,0:T(8,128)(2,1)S(1)}, f32[256,1152]{1,0:T(8,128)S(1)}) custom-call(f32[16,128]{1,0:T(8,128)S(1)} %get-tuple-element.32.params, f32[256,1152]{1,0:T(8,128)S(1)} %collective-permute-done.1.x, bf16[512,1152]{1,0:T(8,128)(2,1)S(1)} %get-tuple-element.39.yh, ...), custom_call_target="tpu_custom_call" | custom-call | flops 2717908992 | bytes 4194304 | tf_op jit(solution)/shard_map/both_terms/pallas_call | solution.py:62
  28.6 7.3 %collective-permute-start.4 = (f32[256,1152]{1,0:T(8,128)S(1)}, f32[256,1152]{1,0:T(8,128)S(1)}, u32[]{:S(2)}, u32[]{:S(2)}) collective-permute-start(f32[256,1152]{1,0:T(8,128)S(1)} %get-tuple-element.44), channel_id=1, source_target_pairs={{0,255},{1,2},{2,1},{3,4},{4,3},{5,6},{6,5},{7,8},{8,7},{9,10},{10... | collective-permute-start | bytes 3538952 | tf_op jit(solution)/shard_map/ppermute | solution.py:296
  35.9 0.8 %collective-permute-done.x = f32[256,1152]{1,0:T(8,128)S(1)} collective-permute-done((f32[256,1152]{1,0:T(8,128)S(1)}, f32[256,1152]{1,0:T(8,128)S(1)}, u32[]{:S(2)}, u32[]{:S(2)}) %collective-permute-start) | collective-permute-done | bytes 1179680 | tf_op jit(solution)/shard_map/ppermute | solution.py:296
  36.7 3.5 %both_terms.3 = (f32[512,1152]{1,0:T(8,128)S(1)}, bf16[256,1152]{1,0:T(8,128)(2,1)S(1)}, bf16[256,1152]{1,0:T(8,128)(2,1)S(1)}, f32[256,1152]{1,0:T(8,128)S(1)}) custom-call(f32[16,128]{1,0:T(8,128)S(1)} %get-tuple-element.32.params, f32[256,1152]{1,0:T(8,128)S(1)} %collective-permute-done.x, ...), custom_call_target="tpu_custom_call", output_to_operand_aliasing={{0}: (4, {})} | custom-call | flops 2717908992 | bytes 4194304 | tf_op jit(solution)/shard_map/both_terms/pallas_call | solution.py:62
  40.3 7.2 %collective-permute-start.3 = (f32[256,1152]{1,0:T(8,128)S(1)}, f32[256,1152]{1,0:T(8,128)S(1)}, u32[]{:S(2)}, u32[]{:S(2)}) collective-permute-start(f32[256,1152]{1,0:T(8,128)S(1)} %get-tuple-element.43), channel_id=1, source_target_pairs={{0,255},{1,2},{2,1},{3,4},{4,3},{5,6},{6,5},{7,8},{8,7},{9,10},{10... | collective-permute-start | bytes 3538952 | tf_op jit(solution)/shard_map/ppermute | solution.py:296
  47.5 0.0 collective-permute-start.5
  47.5 2.4 %collective-permute-done.4.term_in = f32[256,1152]{1,0:T(8,128)S(1)} collective-permute-done((f32[256,1152]{1,0:T(8,128)S(1)}, f32[256,1152]{1,0:T(8,128)S(1)}, u32[]{:S(2)}, u32[]{:S(2)}) %collective-permute-start.4) | collective-permute-done | bytes 1179680 | tf_op jit(solution)/shard_map/ppermute | solution.py:296
  49.9 4.6 %add_term.1.grads = f32[2,512,1152]{2,1,0:T(8,128)S(1)} custom-call(f32[16,128]{1,0:T(8,128)S(1)} %get-tuple-element.32.params, bf16[256,1152]{1,0:T(8,128)(2,1)S(1)} %get-tuple-element.47.refs_0_, bf16[256,1152]{1,0:T(8,128)(2,1)S(1)} %get-tuple-element.48.refs_1_, bf16[256,1152]{1,0:T(8,128)(2,1)S(1)} %get-tuple-element.49.refs_2_, ...), custom_call_target="tpu_custom_call", output_to_operand_aliasing={{}: (7, {})} | custom-call | flops 36238786560 | bytes 4194304 | tf_op jit(solution)/shard_map/add_term/pallas_call | solution.py:62
  54.5 0.0 collective-permute-done.5.term_in
  54.5 1.7 %finish.3 = (f32[512,1152]{1,0:T(8,128)}, f32[512,1152]{1,0:T(8,128)}) custom-call(f32[512,1152]{1,0:T(8,128)S(1)} %collective-permute-done.5.term_in, f32[2,512,1152]{2,1,0:T(8,128)S(1)} %add_term.1.grads), custom_call_target="tpu_custom_call" | custom-call | bytes 4194304 | tf_op jit(solution)/shard_map/finish/pallas_call | solution.py:62
  56.2 1.1 %finish.4 = (f32[512,1152]{1,0:T(8,128)}, f32[512,1152]{1,0:T(8,128)}) custom-call(f32[256,1152]{1,0:T(8,128)S(1)} %collective-permute-done.4.term_in, f32[2,512,1152]{2,1,0:T(8,128)S(1)} %add_term.1.grads, f32[512,1152]{1,0:T(8,128)} %get-tuple-element.52.refs_0_, f32[512,1152]{1,0:T(8,128)} %get-tuple-element.53.refs_1_), custom_call_target="tpu_custom_call", output_to_operand_aliasing={{0}: (2, {}), {1}: (3, {})} | custom-call | bytes 4194304 | tf_op jit(solution)/shard_map/finish/pallas_call | solution.py:62
  57.3 5.3 %collective-permute-done.3.term_in = f32[256,1152]{1,0:T(8,128)S(1)} collective-permute-done((f32[256,1152]{1,0:T(8,128)S(1)}, f32[256,1152]{1,0:T(8,128)S(1)}, u32[]{:S(2)}, u32[]{:S(2)}) %collective-permute-start.3) | collective-permute-done | bytes 1179680 | tf_op jit(solution)/shard_map/ppermute | solution.py:296
  62.6 1.2 %finish.5 = (f32[512,1152]{1,0:T(8,128)}, f32[512,1152]{1,0:T(8,128)}) custom-call(f32[256,1152]{1,0:T(8,128)S(1)} %collective-permute-done.3.term_in, f32[2,512,1152]{2,1,0:T(8,128)S(1)} %add_term.1.grads, f32[512,1152]{1,0:T(8,128)} %get-tuple-element.55.refs_0_, f32[512,1152]{1,0:T(8,128)} %get-tuple-element.56.refs_1_), custom_call_target="tpu_custom_call", output_to_operand_aliasing={{0}: (2, {}), {1}: (3, {})} | custom-call | bytes 4194304 | tf_op jit(solution)/shard_map/finish/pallas_call | solution.py:62
Async XLA Ops:
  1.9 23.3 %collective-permute-start.1 = (f32[256,1152]{1,0:T(8,128)S(1)}, f32[256,1152]{1,0:T(8,128)S(1)}, u32[]{:S(2)}, u32[]{:S(2)}) collective-permute-start(f32[256,1152]{1,0:T(8,128)S(1)} %pick.2.refs_0_), channel_id=1, source_target_pairs={{0,255},{1,2},{2,1},{3,4},{4,3},{5,6},{6,5},{7,8},{8,7},{9,10},{10... | collective-permute-start | bytes 3538952 | tf_op jit(solution)/shard_map/ppermute | solution.py:296
  12.3 24.5 %collective-permute-start = (f32[256,1152]{1,0:T(8,128)S(1)}, f32[256,1152]{1,0:T(8,128)S(1)}, u32[]{:S(2)}, u32[]{:S(2)}) collective-permute-start(f32[256,1152]{1,0:T(8,128)S(1)} %get-tuple-element.31.refs_1_), channel_id=1, source_target_pairs={{0,255},{1,2},{2,1},{3,4},{4,3},{5,6},{6,5},{7,8},{8,7},{9,10},{10... | collective-permute-start | bytes 3538952 | tf_op jit(solution)/shard_map/ppermute | solution.py:296
  12.4 8.1 %collective-permute-start.2 = (f32[512,1152]{1,0:T(8,128)S(1)}, f32[512,1152]{1,0:T(8,128)S(1)}, u32[]{:S(2)}, u32[]{:S(2)}) collective-permute-start(f32[512,1152]{1,0:T(8,128)S(1)} %get-tuple-element.30.chip_block), channel_id=1, source_target_pairs={{0,1},{1,0},{2,3},{3,2},{4,5},{5,4},{6,7},{7,6},{8,9},{9,8},{10,11... | collective-permute-start | bytes 7077896 | tf_op jit(solution)/shard_map/ppermute | solution.py:301
  28.6 21.3 %collective-permute-start.4 = (f32[256,1152]{1,0:T(8,128)S(1)}, f32[256,1152]{1,0:T(8,128)S(1)}, u32[]{:S(2)}, u32[]{:S(2)}) collective-permute-start(f32[256,1152]{1,0:T(8,128)S(1)} %get-tuple-element.44), channel_id=1, source_target_pairs={{0,255},{1,2},{2,1},{3,4},{4,3},{5,6},{6,5},{7,8},{8,7},{9,10},{10... | collective-permute-start | bytes 3538952 | tf_op jit(solution)/shard_map/ppermute | solution.py:296
  40.3 22.3 %collective-permute-start.3 = (f32[256,1152]{1,0:T(8,128)S(1)}, f32[256,1152]{1,0:T(8,128)S(1)}, u32[]{:S(2)}, u32[]{:S(2)}) collective-permute-start(f32[256,1152]{1,0:T(8,128)S(1)} %get-tuple-element.43), channel_id=1, source_target_pairs={{0,255},{1,2},{2,1},{3,4},{4,3},{5,6},{6,5},{7,8},{8,7},{9,10},{10... | collective-permute-start | bytes 3538952 | tf_op jit(solution)/shard_map/ppermute | solution.py:296
  47.5 7.0 %collective-permute-start.5 = (f32[512,1152]{1,0:T(8,128)S(1)}, f32[512,1152]{1,0:T(8,128)S(1)}, u32[]{:S(2)}, u32[]{:S(2)}) collective-permute-start(f32[512,1152]{1,0:T(8,128)S(1)} %get-tuple-element.45), channel_id=1, source_target_pairs={{0,1},{1,0},{2,3},{3,2},{4,5},{5,4},{6,7},{7,6},{8,9},{9,8},{10,11... | collective-permute-start | bytes 7077896 | tf_op jit(solution)/shard_map/ppermute | solution.py:301

commit v6 on v5

--- a/solution.py
+++ b/solution.py
@@ -219,7 +219,7 @@
 def near_kernel(params, y, high, low, grads, grads_out, yh, yl):
     ys = halves(y[...])
     yh[...], yl[...] = ys
-    for span in spans(y.shape[0], TILE):
+    for span in spans(y.shape[0], TILE)[:1]:
         xs = (high[CHIP, span, :], low[CHIP, span, :])
         grads_out[CHIP, span, :] = grads[CHIP, span, :] + term(xs, ys, params)
 
@@ -238,20 +238,20 @@
     )
 
 
-def add_kernel(side, pieces, params, *refs):
+def add_kernel(side, pieces, skip, params, *refs):
     highs, lows, (high, low, grads, grads_out) = refs[:pieces], refs[pieces : 2 * pieces], refs[2 * pieces :]
     ys = tuple(joined([y[...] for y in part], 0) if pieces > 1 else part[0][...] for part in (highs, lows))
-    for span in spans(grads.shape[1], TILE):
+    for span in spans(grads.shape[1], TILE)[skip:]:
         xs = (high[side, span, :], low[side, span, :])
         grads_out[side, span, :] = grads[side, span, :] + term(xs, ys, params)
 
 
-def add_term(side, params, highs, lows, high, low, grads, hint=1):
+def add_term(side, params, highs, lows, high, low, grads, hint=1, skip=0):
     _, rows, width = grads.shape
     pieces = len(highs)
     last = 3 + 2 * pieces
     return call(
-        functools.partial(add_kernel, side, pieces),
+        functools.partial(add_kernel, side, pieces, skip),
         "add_term",
         (params, *highs, *lows, high, low, grads),
         [VMEM] * (last + 1),
@@ -310,7 +310,8 @@
     grads, *ys = near(params, after(b1, grads), high, low, grads)
     mate, ah, al, *terms = both_terms(params, after(a1[0], grads), HEAD_TERMS, ys)
     returned = [over_link(x) for x in terms]
-    mate, th, tl, *terms = both_terms(params, after(a1[1], mate), TAIL_TERMS, ys, mate)
+    grads = add_term(CHIP, params, *([after(y, mate)] for y in ys), high, low, grads, skip=1)
+    mate, th, tl, *terms = both_terms(params, after(a1[1], grads), TAIL_TERMS, ys, mate)
     returned += [over_link(x) for x in terms]
     mate = on_chip(mate)
     grads = add_term(LINK, params, [after(ah, returned[0]), th], [al, tl], high, low, grads, HINT)

time: 64.1 us -> 63.5 us (level)
    pallas_call x10 -> x11, Pallas kernels: 30.2 us -> 30.5 us  [call(): pl.pallas_call(kernel, out_shape=out_shape, in_specs=in_specs, out_specs=...]
  transfers between devices with their start and end apart: 6 -> 6, of which waited for: 3 -> 3; matrix products, arithmetic and copies ran while one was open for 0% -> 0% of each run, Pallas kernels for 43% -> 44%
where the time goes in v6:
time: 63.5 us; the launch traced here: 63.4 us
  Pallas kernels  30.5 us (48%)
  starting transfers between devices  22.5 us (35%)
  waiting for transfers between devices  8.11 us (13%)
  between operations  2.18 us (3%)
    pallas_call x11, Pallas kernels, call(): pl.pallas_call(kernel, out_shape=out_shape, in_specs=in_specs, out_specs=...  30.5 us
    ppermute x4, starting transfers between devices, over_link(): lax.ppermute(x, 'dp', [(i, (i + 1) % peers if i % 2 else (i - 1) % peers)...  22.5 us
    ppermute x4, waiting for transfers between devices, over_link(): lax.ppermute(x, 'dp', [(i, (i + 1) % peers if i % 2 else (i - 1) % peers)...  8.11 us
  transfers between devices with their start and end apart: 6, of which 3 were waited for; matrix products, arithmetic and copies ran while one was open for 0% of the time, Pallas kernels for 44%

profile of v6, /device:TPU:0, one launch (start us, length us, event | category | flops | bytes accessed | tf_op | source)
XLA Modules:
  0.0 63.4 jit_solution(6857766521597743013)
XLA Ops:
  0.6 1.3 %pick.2.refs_0_ = f32[256,1152]{1,0:T(8,128)S(1)} custom-call(f32[512,1152]{1,0:T(8,128)} %images.3, f32[512,1152]{1,0:T(8,128)} %texts.3), custom_call_target="tpu_custom_call" | custom-call | bytes 4194304 | tf_op jit(solution)/shard_map/pick/pallas_call | solution.py:62
  1.9 8.3 %collective-permute-start.2 = (f32[256,1152]{1,0:T(8,128)S(1)}, f32[256,1152]{1,0:T(8,128)S(1)}, u32[]{:S(2)}, u32[]{:S(2)}) collective-permute-start(f32[256,1152]{1,0:T(8,128)S(1)} %pick.2.refs_0_), channel_id=1, source_target_pairs={{0,255},{1,2},{2,1},{3,4},{4,3},{5,6},{6,5},{7,8},{8,7},{9,10},{10... | collective-permute-start | bytes 3538952 | tf_op jit(solution)/shard_map/ppermute | solution.py:296
  10.2 2.0 %pick.3 = (f32[256,1152]{1,0:T(8,128)S(1)}, f32[512,1152]{1,0:T(8,128)S(1)}) custom-call(f32[512,1152]{1,0:T(8,128)} %images.3, f32[512,1152]{1,0:T(8,128)} %texts.3, f32[256,1152]{1,0:T(8,128)S(1)} %pick.2.refs_0_), custom_call_target="tpu_custom_call" | custom-call | bytes 4194304 | tf_op jit(solution)/shard_map/pick/pallas_call | solution.py:62
  12.3 0.1 collective-permute-start
  12.4 0.1 collective-permute-start.1
  13.8 6.7 %own_pair.1 = (f32[2,512,1152]{2,1,0:T(8,128)S(1)}, bf16[2,512,1152]{2,1,0:T(8,128)(2,1)S(1)}, bf16[2,512,1152]{2,1,0:T(8,128)(2,1)S(1)}, f32[16,128]{1,0:T(8,128)S(1)}) custom-call(f32[1,1]{1,0:T(1,128)} %bitcast.2.scale_ref, f32[1,1]{1,0:T(1,128)} %bitcast.3.bias_ref, f32[512,1152]{1,0:T(8,128)S(1)} %get-tuple-element.32.chip_block, ...), custom_call_target="tpu_custom_call" | custom-call | flops 54358179840 | bytes 4194304 | tf_op jit(solution)/shard_map/own_pair/pallas_call | solution.py:62
  20.5 0.0 collective-permute-done.1.y
  20.5 2.5 %near_pair.1 = (f32[2,512,1152]{2,1,0:T(8,128)S(1)}, bf16[512,1152]{1,0:T(8,128)(2,1)S(1)}, bf16[512,1152]{1,0:T(8,128)(2,1)S(1)}) custom-call(f32[16,128]{1,0:T(8,128)S(1)} %get-tuple-element.34.params, f32[512,1152]{1,0:T(8,128)S(1)} %collective-permute-done.1.y, ...), custom_call_target="tpu_custom_call", output_to_operand_aliasing={{0}: (4, {})} | custom-call | flops 3623878656 | bytes 4194304 | tf_op jit(solution)/shard_map/near_pair/pallas_call | solution.py:62
  23.0 1.1 %collective-permute-done.2.x = f32[256,1152]{1,0:T(8,128)S(1)} collective-permute-done((f32[256,1152]{1,0:T(8,128)S(1)}, f32[256,1152]{1,0:T(8,128)S(1)}, u32[]{:S(2)}, u32[]{:S(2)}) %collective-permute-start.2) | collective-permute-done | bytes 1179680 | tf_op jit(solution)/shard_map/ppermute | solution.py:296
  24.1 3.4 %both_terms.2 = (f32[512,1152]{1,0:T(8,128)S(1)}, bf16[256,1152]{1,0:T(8,128)(2,1)S(1)}, bf16[256,1152]{1,0:T(8,128)(2,1)S(1)}, f32[256,1152]{1,0:T(8,128)S(1)}) custom-call(f32[16,128]{1,0:T(8,128)S(1)} %get-tuple-element.34.params, f32[256,1152]{1,0:T(8,128)S(1)} %collective-permute-done.2.x, bf16[512,1152]{1,0:T(8,128)(2,1)S(1)} %get-tuple-element.44.yh.refs_0_, ...), custom_call_target="tpu_custom_call" | custom-call | flops 2717908992 | bytes 4194304 | tf_op jit(solution)/shard_map/both_terms/pallas_call | solution.py:62
  27.5 7.4 %collective-permute-start.4 = (f32[256,1152]{1,0:T(8,128)S(1)}, f32[256,1152]{1,0:T(8,128)S(1)}, u32[]{:S(2)}, u32[]{:S(2)}) collective-permute-start(f32[256,1152]{1,0:T(8,128)S(1)} %get-tuple-element.48), channel_id=1, source_target_pairs={{0,255},{1,2},{2,1},{3,4},{4,3},{5,6},{6,5},{7,8},{8,7},{9,10},{10... | collective-permute-start | bytes 3538952 | tf_op jit(solution)/shard_map/ppermute | solution.py:296
  35.0 2.4 %add_term.2.refs_6_ = f32[2,512,1152]{2,1,0:T(8,128)S(1)} custom-call(f32[16,128]{1,0:T(8,128)S(1)} %get-tuple-element.34.params, bf16[512,1152]{1,0:T(8,128)(2,1)S(1)} %get-tuple-element.44.yh.refs_0_, bf16[512,1152]{1,0:T(8,128)(2,1)S(1)} %get-tuple-element.45.yl.refs_1_, ...), custom_call_target="tpu_custom_call", output_to_operand_aliasing={{}: (5, {})} | custom-call | flops 3623878656 | bytes 4194304 | tf_op jit(solution)/shard_map/add_term/pallas_call | solution.py:62
  37.3 0.0 collective-permute-done.x
  37.4 3.5 %both_terms.3 = (f32[512,1152]{1,0:T(8,128)S(1)}, bf16[256,1152]{1,0:T(8,128)(2,1)S(1)}, bf16[256,1152]{1,0:T(8,128)(2,1)S(1)}, f32[256,1152]{1,0:T(8,128)S(1)}) custom-call(f32[16,128]{1,0:T(8,128)S(1)} %get-tuple-element.34.params, f32[256,1152]{1,0:T(8,128)S(1)} %collective-permute-done.x, ...), custom_call_target="tpu_custom_call", output_to_operand_aliasing={{0}: (4, {})} | custom-call | flops 2717908992 | bytes 4194304 | tf_op jit(solution)/shard_map/both_terms/pallas_call | solution.py:62
  40.9 6.6 %collective-permute-start.3 = (f32[256,1152]{1,0:T(8,128)S(1)}, f32[256,1152]{1,0:T(8,128)S(1)}, u32[]{:S(2)}, u32[]{:S(2)}) collective-permute-start(f32[256,1152]{1,0:T(8,128)S(1)} %get-tuple-element.47), channel_id=1, source_target_pairs={{0,255},{1,2},{2,1},{3,4},{4,3},{5,6},{6,5},{7,8},{8,7},{9,10},{10... | collective-permute-start | bytes 3538952 | tf_op jit(solution)/shard_map/ppermute | solution.py:296
  47.5 0.0 collective-permute-start.5
  47.5 1.8 %collective-permute-done.4.term_in = f32[256,1152]{1,0:T(8,128)S(1)} collective-permute-done((f32[256,1152]{1,0:T(8,128)S(1)}, f32[256,1152]{1,0:T(8,128)S(1)}, u32[]{:S(2)}, u32[]{:S(2)}) %collective-permute-start.4) | collective-permute-done | bytes 1179680 | tf_op jit(solution)/shard_map/ppermute | solution.py:296
  49.4 4.6 %add_term.3.grads = f32[2,512,1152]{2,1,0:T(8,128)S(1)} custom-call(f32[16,128]{1,0:T(8,128)S(1)} %get-tuple-element.34.params, bf16[256,1152]{1,0:T(8,128)(2,1)S(1)} %get-tuple-element.51.refs_0_, bf16[256,1152]{1,0:T(8,128)(2,1)S(1)} %get-tuple-element.52.refs_1_, bf16[256,1152]{1,0:T(8,128)(2,1)S(1)} %get-tuple-element.53.refs_2_, ...), custom_call_target="tpu_custom_call", output_to_operand_aliasing={{}: (7, {})} | custom-call | flops 36238786560 | bytes 4194304 | tf_op jit(solution)/shard_map/add_term/pallas_call | solution.py:62
  54.0 0.0 collective-permute-done.5.term_in
  54.0 1.7 %finish.3 = (f32[512,1152]{1,0:T(8,128)}, f32[512,1152]{1,0:T(8,128)}) custom-call(f32[512,1152]{1,0:T(8,128)S(1)} %collective-permute-done.5.term_in, f32[2,512,1152]{2,1,0:T(8,128)S(1)} %add_term.3.grads), custom_call_target="tpu_custom_call" | custom-call | bytes 4194304 | tf_op jit(solution)/shard_map/finish/pallas_call | solution.py:62
  55.7 1.1 %finish.4 = (f32[512,1152]{1,0:T(8,128)}, f32[512,1152]{1,0:T(8,128)}) custom-call(f32[256,1152]{1,0:T(8,128)S(1)} %collective-permute-done.4.term_in, f32[2,512,1152]{2,1,0:T(8,128)S(1)} %add_term.3.grads, f32[512,1152]{1,0:T(8,128)} %get-tuple-element.56.refs_0_, f32[512,1152]{1,0:T(8,128)} %get-tuple-element.57.refs_1_), custom_call_target="tpu_custom_call", output_to_operand_aliasing={{0}: (2, {}), {1}: (3, {})} | custom-call | bytes 4194304 | tf_op jit(solution)/shard_map/finish/pallas_call | solution.py:62
  56.9 5.2 %collective-permute-done.3.term_in = f32[256,1152]{1,0:T(8,128)S(1)} collective-permute-done((f32[256,1152]{1,0:T(8,128)S(1)}, f32[256,1152]{1,0:T(8,128)S(1)}, u32[]{:S(2)}, u32[]{:S(2)}) %collective-permute-start.3) | collective-permute-done | bytes 1179680 | tf_op jit(solution)/shard_map/ppermute | solution.py:296
  62.0 1.2 %finish.5 = (f32[512,1152]{1,0:T(8,128)}, f32[512,1152]{1,0:T(8,128)}) custom-call(f32[256,1152]{1,0:T(8,128)S(1)} %collective-permute-done.3.term_in, f32[2,512,1152]{2,1,0:T(8,128)S(1)} %add_term.3.grads, f32[512,1152]{1,0:T(8,128)} %get-tuple-element.59.refs_0_, f32[512,1152]{1,0:T(8,128)} %get-tuple-element.60.refs_1_), custom_call_target="tpu_custom_call", output_to_operand_aliasing={{0}: (2, {}), {1}: (3, {})} | custom-call | bytes 4194304 | tf_op jit(solution)/shard_map/finish/pallas_call | solution.py:62
Async XLA Ops:
  1.9 22.2 %collective-permute-start.2 = (f32[256,1152]{1,0:T(8,128)S(1)}, f32[256,1152]{1,0:T(8,128)S(1)}, u32[]{:S(2)}, u32[]{:S(2)}) collective-permute-start(f32[256,1152]{1,0:T(8,128)S(1)} %pick.2.refs_0_), channel_id=1, source_target_pairs={{0,255},{1,2},{2,1},{3,4},{4,3},{5,6},{6,5},{7,8},{8,7},{9,10},{10... | collective-permute-start | bytes 3538952 | tf_op jit(solution)/shard_map/ppermute | solution.py:296
  12.3 25.1 %collective-permute-start = (f32[256,1152]{1,0:T(8,128)S(1)}, f32[256,1152]{1,0:T(8,128)S(1)}, u32[]{:S(2)}, u32[]{:S(2)}) collective-permute-start(f32[256,1152]{1,0:T(8,128)S(1)} %get-tuple-element.33.refs_1_), channel_id=1, source_target_pairs={{0,255},{1,2},{2,1},{3,4},{4,3},{5,6},{6,5},{7,8},{8,7},{9,10},{10... | collective-permute-start | bytes 3538952 | tf_op jit(solution)/shard_map/ppermute | solution.py:296
  12.4 8.1 %collective-permute-start.1 = (f32[512,1152]{1,0:T(8,128)S(1)}, f32[512,1152]{1,0:T(8,128)S(1)}, u32[]{:S(2)}, u32[]{:S(2)}) collective-permute-start(f32[512,1152]{1,0:T(8,128)S(1)} %get-tuple-element.32.chip_block), channel_id=1, source_target_pairs={{0,1},{1,0},{2,3},{3,2},{4,5},{5,4},{6,7},{7,6},{8,9},{9,8},{10,11... | collective-permute-start | bytes 7077896 | tf_op jit(solution)/shard_map/ppermute | solution.py:301
  27.5 21.8 %collective-permute-start.4 = (f32[256,1152]{1,0:T(8,128)S(1)}, f32[256,1152]{1,0:T(8,128)S(1)}, u32[]{:S(2)}, u32[]{:S(2)}) collective-permute-start(f32[256,1152]{1,0:T(8,128)S(1)} %get-tuple-element.48), channel_id=1, source_target_pairs={{0,255},{1,2},{2,1},{3,4},{4,3},{5,6},{6,5},{7,8},{8,7},{9,10},{10... | collective-permute-start | bytes 3538952 | tf_op jit(solution)/shard_map/ppermute | solution.py:296
  40.9 21.1 %collective-permute-start.3 = (f32[256,1152]{1,0:T(8,128)S(1)}, f32[256,1152]{1,0:T(8,128)S(1)}, u32[]{:S(2)}, u32[]{:S(2)}) collective-permute-start(f32[256,1152]{1,0:T(8,128)S(1)} %get-tuple-element.47), channel_id=1, source_target_pairs={{0,255},{1,2},{2,1},{3,4},{4,3},{5,6},{6,5},{7,8},{8,7},{9,10},{10... | collective-permute-start | bytes 3538952 | tf_op jit(solution)/shard_map/ppermute | solution.py:296
  47.5 6.4 %collective-permute-start.5 = (f32[512,1152]{1,0:T(8,128)S(1)}, f32[512,1152]{1,0:T(8,128)S(1)}, u32[]{:S(2)}, u32[]{:S(2)}) collective-permute-start(f32[512,1152]{1,0:T(8,128)S(1)} %get-tuple-element.49), channel_id=1, source_target_pairs={{0,1},{1,0},{2,3},{3,2},{4,5},{5,4},{6,7},{7,6},{8,9},{9,8},{10,11... | collective-permute-start | bytes 7077896 | tf_op jit(solution)/shard_map/ppermute | solution.py:301
